TPU v7x, 512 devices: a whole 4x4x16 slice. The times are simulated.
512 devices in a mesh: row: 16 (over y, x_lo, core), col: 32 (over x_hi, z).
Axes of the slice: x: 4 (x_hi: 2, x_lo: 2; x = x_hi * 2 + x_lo), y: 4, z: 16, core: 2. Of those that a mesh axis runs over, the one named last changes fastest.
Arguments:
- pair: bfloat16 [768, 768, 128], P('row', 'col'), may hold values from -6 to 6
- pair_mask: int32 [768, 768], P('row', 'col'), may hold values from 0 to 1, as said below
- weights: bfloat16 [6, 128, 128], replicated, may hold values from -0.5 to 0.5
- cotangent: bfloat16 [768, 768, 128], P('row', 'col'), may hold values from -6 to 6
Outputs:
- update: bfloat16 [768, 768, 128], P('row', 'col')
- grad_pair: float32 [768, 768, 128], P('row', 'col')
- grad_weights: float32 [6, 128, 128], replicated
Inputs may be any that keep to these rules, and one draw needn't show every extreme that they name: pair_mask[i, j] = m_i m_j with a residue mask m of 0 and 1: m_i is 0 for every residue at or past a padding length L, 576 <= L < 768, and for some residues before it.
All inputs are finite; a program needn't handle non-finite values.
Results may differ from a plain program's by a relative error of at most 0.012.
Values may be sent and summed in bfloat16 or wider, within the bound.
A program may use at most 64 MiB of HBM per device.

v0:
```python
import jax
import jax.numpy as jnp
from jax import lax
from jax.sharding import PartitionSpec as P


def normalize(values):
    average = jnp.mean(values, axis=-1, keepdims=True)
    centred = values - average
    variance = jnp.mean(centred * centred, axis=-1, keepdims=True)
    inverse = lax.rsqrt(variance + 1e-05)
    return (centred * inverse, inverse)


def norm_backward(upstream, normed, inverse):
    first = jnp.mean(upstream, axis=-1, keepdims=True)
    second = jnp.mean(upstream * normed, axis=-1, keepdims=True)
    return inverse * (upstream - first - normed * second)


def on_device(pair, pair_mask, weights, cotangent):
    row_count, col_count, channels = pair.shape
    residues = row_count * lax.axis_size("row")
    pixels = row_count * col_count
    normed_in, inv_in = normalize(pair.astype(jnp.float32))
    flat_in = normed_in.astype(jnp.bfloat16).reshape(pixels, channels)
    weight_in = jnp.concatenate([weights[number] for number in range(5)], axis=1)
    projected_all = jnp.dot(flat_in, weight_in, preferred_element_type=jnp.float32).reshape(
        row_count, col_count, 5 * channels
    )
    projected = [
        projected_all[..., number * channels : (number + 1) * channels] for number in range(5)
    ]
    mask_float = pair_mask.astype(jnp.float32)[..., None]
    left_sig = jax.nn.sigmoid(projected[1])
    right_sig = jax.nn.sigmoid(projected[3])
    left_act = (mask_float * left_sig * projected[0]).astype(jnp.bfloat16)
    right_act = (mask_float * right_sig * projected[2]).astype(jnp.bfloat16)
    left_chan, right_chan = (
        lax.all_to_all(left_act.transpose(2, 0, 1), "col", split_axis=0, concat_axis=2, tiled=True),
        lax.all_to_all(
            right_act.transpose(2, 0, 1), "col", split_axis=0, concat_axis=2, tiled=True
        ),
    )
    right_full = lax.all_gather(right_chan, "row", axis=1, tiled=True)
    tri_chan = jnp.einsum(
        "cik,cjk->cij", left_chan, right_full, preferred_element_type=jnp.float32
    ).astype(jnp.bfloat16)
    tri_tile = lax.all_to_all(tri_chan, "col", split_axis=2, concat_axis=0, tiled=True)
    normed_out, inv_out = normalize(tri_tile.transpose(1, 2, 0).astype(jnp.float32))
    flat_out = normed_out.astype(jnp.bfloat16).reshape(pixels, channels)
    linear = jnp.dot(flat_out, weights[5], preferred_element_type=jnp.float32).reshape(
        row_count, col_count, channels
    )
    gate_sig = jax.nn.sigmoid(projected[4])
    update = (gate_sig * linear).astype(jnp.bfloat16)
    upstream = cotangent.astype(jnp.float32)
    grad_linear = (upstream * gate_sig).astype(jnp.bfloat16)
    grad_logit = (upstream * linear * gate_sig * (1.0 - gate_sig)).astype(jnp.bfloat16)
    linear_flat = grad_linear.reshape(pixels, channels)
    grad_xout = jnp.dot(linear_flat, weights[5].T, preferred_element_type=jnp.float32).reshape(
        row_count, col_count, channels
    )
    grad_tri = norm_backward(grad_xout, normed_out, inv_out).astype(jnp.bfloat16)
    grad_chan = lax.all_to_all(
        grad_tri.transpose(2, 0, 1), "col", split_axis=0, concat_axis=2, tiled=True
    )
    left_grad_chan = jnp.einsum(
        "cij,cjk->cik", grad_chan, right_full, preferred_element_type=jnp.float32
    ).astype(jnp.bfloat16)
    own_start = lax.axis_index("row") * row_count
    grad_piece = lax.all_gather(grad_chan, "row", axis=1, tiled=True)
    left_piece = lax.all_gather(left_chan, "row", axis=1, tiled=True)
    selected = lax.dynamic_slice_in_dim(grad_piece, own_start, row_count, 2)
    right_grad_chan = jnp.einsum(
        "cij,cik->cjk", selected, left_piece, preferred_element_type=jnp.float32
    ).astype(jnp.bfloat16)
    left_back, right_back = (
        lax.all_to_all(left_grad_chan, "col", split_axis=2, concat_axis=0, tiled=True),
        lax.all_to_all(right_grad_chan, "col", split_axis=2, concat_axis=0, tiled=True),
    )
    left_float = left_back.transpose(1, 2, 0).astype(jnp.float32) * mask_float
    right_float = right_back.transpose(1, 2, 0).astype(jnp.float32) * mask_float
    grads = [
        (left_float * left_sig).astype(jnp.bfloat16),
        (left_float * projected[0] * left_sig * (1.0 - left_sig)).astype(jnp.bfloat16),
        (right_float * right_sig).astype(jnp.bfloat16),
        (right_float * projected[2] * right_sig * (1.0 - right_sig)).astype(jnp.bfloat16),
        grad_logit,
    ]
    grad_stack = jnp.concatenate(grads, axis=-1).reshape(pixels, 5 * channels)
    grad_xin = jnp.dot(grad_stack, weight_in.T, preferred_element_type=jnp.float32).reshape(
        row_count, col_count, channels
    )
    grad_pair = norm_backward(grad_xin, normed_in, inv_in)
    input_terms = jnp.einsum("pc,pd->cd", flat_in, grad_stack, preferred_element_type=jnp.float32)
    output_terms = jnp.einsum(
        "pc,pd->cd", flat_out, linear_flat, preferred_element_type=jnp.float32
    )
    input_total, output_total = lax.psum((input_terms, output_terms), ("row", "col"))
    weight_list = [
        input_total[:, number * channels : (number + 1) * channels] for number in range(5)
    ]
    weight_list.append(output_total)
    grad_weights = jnp.stack(weight_list) / jnp.float32(residues)
    return (update, grad_pair, grad_weights)


def solution(mesh):
    placed = (P("row", "col", None), P("row", "col"), P(), P("row", "col", None))
    return jax.shard_map(
        on_device,
        mesh=mesh,
        in_specs=placed,
        out_specs=(P("row", "col", None), P("row", "col", None), P()),
        check_vma=False,
    )
```

profile of v0, /device:TPU:1, one launch (start us, length us, event | category | flops | bytes accessed | tf_op | source)
XLA Modules:
  0.0 831.1 jit_solution(3977221925135359949)
XLA Ops:
  21.0 41.0 %all_to_all.81 = bf16[32,2,2304]{2,1,0:T(2,128)(2,1)} all-to-all(bf16[32,2,2304]{2,1,0:T(2,128)(2,1)S(1)} %reshape.93), channel_id=1, replica_groups=mesh['row'=16,'col'=32] {'col'}, dimensions={0} | all-to-all | bytes 589824 | tf_op jit(solution)/shard_map/all_to_all | solution.py:41
  62.0 3.0 reshape.94
  73.0 27.7 %all_to_all.82 = bf16[32,2,2304]{2,1,0:T(2,128)(2,1)S(1)} all-to-all(bf16[32,2,2304]{2,1,0:T(2,128)(2,1)S(1)} %reshape.91), channel_id=1, replica_groups=mesh['row'=16,'col'=32] {'col'}, dimensions={0} | all-to-all | bytes 589824 | tf_op jit(solution)/shard_map/all_to_all | solution.py:40
  104.5 5.3 all-gather.4.cloned.1.call-done
  109.8 4.1 convolution_convert_fusion.2
  115.1 2.7 reshape.95
  117.8 37.8 %all_to_all.83 = bf16[32,2,2304]{2,1,0:T(2,128)(2,1)S(1)} all-to-all(bf16[32,2,2304]{2,1,0:T(2,128)(2,1)S(1)} %reshape.95), channel_id=1, replica_groups=mesh['row'=16,'col'=32] {'col'}, dimensions={0} | all-to-all | bytes 589824 | tf_op jit(solution)/shard_map/all_to_all | solution.py:49
  168.2 3.0 reshape.97
  171.2 25.7 %all_to_all.84 = bf16[32,2,2304]{2,1,0:T(2,128)(2,1)} all-to-all(bf16[32,2,2304]{2,1,0:T(2,128)(2,1)} %reshape.97), channel_id=1, replica_groups=mesh['row'=16,'col'=32] {'col'}, dimensions={0} | all-to-all | bytes 589824 | tf_op jit(solution)/shard_map/all_to_all | solution.py:65
  196.9 3.0 reshape.98
  206.3 4.3 convolution_convert_fusion.1
  212.7 3.3 reshape.99
  216.0 6.7 all-to-all-start.4
  222.7 22.1 %all-gather.6.cloned.1.call-done = bf16[4,768,768]{2,0,1:T(4,128)(2,1)} async-done(((bf16[4,48,768]{2,0,1:T(4,128)(2,1)}), bf16[4,768,768]{2,0,1:T(4,128)(2,1)}) %all-gather.6.cloned.1.call-update) | async-done | bytes 4718608 | tf_op jit(solution)/shard_map/all_gather | solution.py:72
  244.8 2.9 constant_dynamic-slice_fusion
  247.6 46.9 %all-gather.8.cloned.1.call-done = bf16[4,768,768]{2,1,0:T(8,128)(2,1)} async-done(((bf16[4,48,768]{2,1,0:T(8,128)(2,1)}), bf16[4,768,768]{2,1,0:T(8,128)(2,1)}) %all-gather.8.cloned.1.call-update) | async-done | bytes 4718608 | tf_op jit(solution)/shard_map/all_gather | solution.py:73
  294.5 4.3 convolution_convert_fusion
  300.9 3.3 reshape.101
  304.2 14.6 %all-to-all-start.5 = ((bf16[32,2,2304]{2,1,0:T(2,128)(2,1)}), bf16[32,2,2304]{2,1,0:T(2,128)(2,1)}, u32[]{:S(2)}, u32[]{:S(2)}) async-start(bf16[32,2,2304]{2,1,0:T(2,128)(2,1)} %reshape.101), calls=%async_computation.5 | async-start | bytes 589824 | tf_op jit(solution)/shard_map/all_to_all | solution.py:80
  323.4 3.5 reshape.100
  334.9 7.4 all-to-all-done.5
  342.3 3.5 reshape.102
  356.1 3.0 convolution_bitcast_fusion
  362.7 456.0 %all-reduce.3.cloned.1.call-done = (f32[128,640]{1,0:T(8,128)}, f32[1,128,128]{2,1,0:T(8,128)}) async-done(((f32[128,640]{1,0:T(8,128)}, f32[1,128,128]{2,1,0:T(8,128)}), (f32[128,640]{1,0:T(8,128)}, f32[1,128,128]{2,1,0:T(8,128)})) %all-reduce.3.cloned.1.call-update) | async-done | bytes 393232 | tf_op jit(solution)/shard_map/psum | solution.py:100
  (105 shorter events, 82.1 us)
Async XLA Ops:
  7.2 102.6 %all-gather.4.cloned.1.call-start = ((), (), s32[]{:S(2)}) async-start(), calls=%async_computation.6 | async-start | bytes 5013504 | tf_op jit(solution)/shard_map/all_gather | solution.py:45
  8.4 6.7 copy-start.3
  9.8 5.3 copy-start.6
  13.7 1.4 copy-start.9
  15.1 1.8 copy-start.2
  69.2 175.6 %all-gather.6.cloned.1.call-start = ((), (), s32[]{:S(2)}) async-start(), calls=%async_computation.7 | async-start | bytes 5013504 | tf_op jit(solution)/shard_map/all_gather | solution.py:72
  162.2 2.2 copy-start.11
  162.6 1.7 copy-start.13
  204.2 90.4 %all-gather.8.cloned.1.call-start = ((), (), s32[]{:S(2)}) async-start(), calls=%async_computation.8 | async-start | bytes 5013504 | tf_op jit(solution)/shard_map/all_gather | solution.py:73
  216.0 88.2 %all-to-all-start.4 = ((bf16[32,2,2304]{2,1,0:T(2,128)(2,1)}), bf16[32,2,2304]{2,1,0:T(2,128)(2,1)}, u32[]{:S(2)}, u32[]{:S(2)}) async-start(bf16[32,2,2304]{2,1,0:T(2,128)(2,1)} %reshape.99), calls=%async_computation.4 | async-start | bytes 589824 | tf_op jit(solution)/shard_map/all_to_all | solution.py:79
  304.2 38.1 %all-to-all-start.5 = ((bf16[32,2,2304]{2,1,0:T(2,128)(2,1)}), bf16[32,2,2304]{2,1,0:T(2,128)(2,1)}, u32[]{:S(2)}, u32[]{:S(2)}) async-start(bf16[32,2,2304]{2,1,0:T(2,128)(2,1)} %reshape.101), calls=%async_computation.5 | async-start | bytes 589824 | tf_op jit(solution)/shard_map/all_to_all | solution.py:80
  318.8 499.9 %all-reduce.3.cloned.1.call-start = ((), (), s32[]{:S(2)}) async-start(), calls=%async_computation.9 | async-start | bytes 786432 | tf_op jit(solution)/shard_map/psum | solution.py:100
  318.9 2.3 copy-start.12
  318.9 2.3 copy-start.14
  350.4 0.8 copy-start.1
  351.2 3.9 copy-start.5
  351.2 3.9 copy-start.8
  353.0 3.1 copy-start
  353.0 3.1 copy-start.4
  353.0 3.1 copy-start.7
  355.1 3.9 copy-start.10
Sparse Core Ops, SparseCore 0:
  69.3 40.3 all-gather.3
  204.3 40.4 all-gather.5
  247.5 47.0 all-gather.7
  361.3 457.3 all-reduce.2
where the time goes:
time: 834 us; the launch traced here: 831 us
  waiting for transfers between devices  538 us (65%)
  blocking collectives  132 us (16%)
  local copies, waits for them, and re-layouts  83.4 us (10%)
  matrix products  25.7 us (3%)
  starting transfers between devices  21.5 us (3%)
  other arithmetic  16.6 us (2%)
  between operations  14.1 us (2%)
    psum x1, waiting for transfers between devices, on_device(): lax.psum((input_terms, output_terms), ('row', 'col'))  456 us
    all_gather x1, waiting for transfers between devices, on_device(): left_piece = lax.all_gather(left_chan, 'row', axis=1, tiled=True)  46.9 us
    unnamed x51, local copies, waits for them, and re-layouts  41.7 us
    all_to_all x1, blocking collectives, on_device(): lax.all_to_all(right_act.transpose(2, 0, 1), 'col', split_axis=0, concat_...  41 us
    all_to_all x1, blocking collectives, on_device(): lax.all_to_all(tri_chan, 'col', split_axis=2, concat_axis=0, tiled=True)  37.8 us
    all_to_all x1, blocking collectives, on_device(): lax.all_to_all(left_act.transpose(2, 0, 1), 'col', split_axis=0, concat_a...  27.7 us
    all_to_all x1, blocking collectives, on_device(): lax.all_to_all(grad_tri.transpose(2, 0, 1), 'col', split_axis=0, concat_a...  25.7 us
    all_gather x1, waiting for transfers between devices, on_device(): grad_piece = lax.all_gather(grad_chan, 'row', axis=1, tiled=True)  22.1 us
  transfers between devices with their start and end apart: 6, of which 5 were waited for; matrix products, arithmetic and copies ran while one was open for 6% of the time, Pallas kernels for 0%

commit v1 on v0

v1 whole, which is shorter than its diff:
```python
import functools

import jax
import jax.numpy as jnp
import numpy as np
from jax import lax
from jax.experimental import pallas as pl
from jax.experimental.pallas import tpu as pltpu
from jax.sharding import PartitionSpec as P


F32 = jnp.float32
BF16 = jnp.bfloat16
C = 128
BLOCKS = 9
Y, S, Q, R = 4, 4, 32, 16
ROWS = 192
WIDE = 1024
PAIRED, SINGLE = 80, 48
MESH = pl.DeviceIdType.MESH


def nt(a, b):
    return lax.dot_general(a, b, (((1,), (1,)), ((), ())), preferred_element_type=F32)


def nn(a, b):
    return lax.dot_general(a, b, (((1,), (0,)), ((), ())), preferred_element_type=F32)


def tn(a, b):
    return lax.dot_general(a, b, (((0,), (0,)), ((), ())), preferred_element_type=F32)


def normalize(values):
    average = jnp.mean(values, axis=0, keepdims=True)
    centred = values - average
    variance = jnp.mean(centred * centred, axis=0, keepdims=True)
    inverse = lax.rsqrt(variance + 1e-05)
    return centred * inverse, inverse


def norm_backward(upstream, normed, inverse):
    first = jnp.mean(upstream, axis=0, keepdims=True)
    second = jnp.mean(upstream * normed, axis=0, keepdims=True)
    return inverse * (upstream - first - normed * second)


def column_order():
    low, block, tile = np.meshgrid(np.arange(8), np.arange(3), np.arange(Q), indexing="ij")
    residue = (tile * 24 + block * 8 + low).reshape(-1)
    place = (low * 128 + block * 32 + tile).reshape(-1)
    y, s, inner = residue // 192, residue // 48 % 4, residue % 48
    order = np.zeros((S, WIDE, 256), np.float32)
    order[s, place, y * 48 + inner] = 1
    return order.astype(jnp.bfloat16)


def loop(count, body):
    def step(i, carry):
        body(i)
        return carry

    lax.fori_loop(0, count, step, 0)


def kernel(
    pair_ref,
    cot_ref,
    mask_ref,
    win_ref,
    wback_ref,
    wout_ref,
    woutb_ref,
    order_ref,
    upd_ref,
    gpair_ref,
    gw_ref,
    proj,
    xn,
    xb,
    inv,
    logit,
    flat,
    ys_a,
    yr_a,
    zs_a,
    zr_a,
    ys_t,
    yr_t,
    zs_t,
    zr_t,
    ys_g,
    yr_g,
    zs_g,
    zr_g,
    ys_b,
    yr_b,
    zs_b,
    zr_b,
    left,
    right,
    gmat,
    acc,
    gs,
    gr,
    gw5,
    gwin,
    wfull,
    ws1,
    wr1,
    ws2,
    wr2,
    ws3,
    wr3,
    y_send,
    y_recv,
    z_send,
    z_recv,
    s_send,
    s_recv,
    w1_send,
    w1_recv,
    w2_send,
    w2_recv,
    w3_send,
    w3_recv,
):
    r = lax.axis_index("row")
    q = lax.axis_index("col")
    y = r // 4
    s = r % 4
    barrier = pltpu.get_barrier_semaphore()

    def signal_col(d):
        pl.semaphore_signal(
            barrier, inc=1, device_id={"row": r, "col": (q + 1 + d) % Q}, device_id_type=MESH
        )

    def signal_row(d):
        pl.semaphore_signal(
            barrier, inc=1, device_id={"row": (r + 1 + d) % R, "col": q}, device_id_type=MESH
        )

    loop(Q - 1, signal_col)
    loop(R - 1, signal_row)

    def partner(step):
        u = Q - 1 - step
        t = u // 2
        hop = ((t + 1) // 2) * (2 * (t % 2) - 1)
        z = (q % 16 + hop + 16) % 16
        return ((q // 16 + u) % 2) * 16 + z

    def y_copy(phase, src, dst, d):
        to = (y + 1 + d) % Y
        return pltpu.make_async_remote_copy(
            src_ref=src.at[to],
            dst_ref=dst.at[y],
            send_sem=y_send.at[phase, to],
            recv_sem=y_recv.at[phase, y],
            device_id={"row": to * 4 + s, "col": q},
            device_id_type=MESH,
        )

    def y_wait(phase, src, dst, d):
        frm = (y + 1 + d) % Y
        pltpu.make_async_remote_copy(
            src_ref=src.at[frm],
            dst_ref=dst.at[frm],
            send_sem=y_send.at[phase, frm],
            recv_sem=y_recv.at[phase, frm],
            device_id={"row": frm * 4 + s, "col": q},
            device_id_type=MESH,
        ).wait_recv()

    def y_exchange(phase, src, dst):
        loop(Y - 1, lambda d: y_copy(phase, src, dst, d).start())
        dst[y] = src[y]
        loop(Y - 1, lambda d: y_wait(phase, src, dst, d))

    def z_copy(phase, src, dst, to):
        return pltpu.make_async_remote_copy(
            src_ref=src.at[to],
            dst_ref=dst.at[q],
            send_sem=z_send.at[phase, to],
            recv_sem=z_recv.at[phase, q],
            device_id={"row": r, "col": to},
            device_id_type=MESH,
        )

    def z_exchange(phase, src, dst, rows, make):
        def send(step):
            to = partner(step)
            src[to] = make(to)
            z_copy(phase, src, dst, to).start()

        def receive(step):
            frm = partner(Q - 2 - step)
            pltpu.make_async_remote_copy(
                src_ref=src.at[frm],
                dst_ref=dst.at[frm],
                send_sem=z_send.at[phase, frm],
                recv_sem=z_recv.at[phase, frm],
                device_id={"row": r, "col": frm},
                device_id_type=MESH,
            ).wait_recv()
            flat[pl.ds(pl.multiple_of(frm * rows, 16), rows), :] = dst[frm].astype(F32)

        loop(Q - 1, send)
        dst[q] = make(q)
        flat[pl.ds(pl.multiple_of(q * rows, 16), rows), :] = dst[q].astype(F32)
        loop(Q - 1, receive)

    def spread(arrays, recv):
        def body(step):
            yy, block = step // (arrays * BLOCKS), step % (arrays * BLOCKS)
            row = (block // BLOCKS) * 36 + yy * BLOCKS + block % BLOCKS
            flat[pl.ds(pl.multiple_of(row * 32, 32), 32), :] = recv[yy, block].astype(F32)

        loop(Y * arrays * BLOCKS, body)

    def pick(rows):
        return lambda to: flat[pl.ds(to, rows, stride=32), :].astype(BF16)

    def stored(rows):
        return lambda to: flat[pl.ds(pl.multiple_of(to * rows, 16), rows), :].astype(BF16)

    def gather_up(arrays, rows, send):
        def body(step):
            yy, block = step // (arrays * BLOCKS), step % (arrays * BLOCKS)
            row = (block // BLOCKS) * 36 + yy * BLOCKS + block % BLOCKS
            send[yy, block] = flat[pl.ds(row, Q, stride=rows), :].astype(BF16)

        loop(Y * arrays * BLOCKS, body)

    def to_matrix(first, rows, write):
        def body(step):
            parts = [flat[pl.ds(first + 3 * step + b, Q, stride=rows), :] for b in range(3)]
            turned = jnp.concatenate(parts + [jnp.zeros((Q, C), F32)], axis=0).T.astype(BF16)
            for low in range(8):
                write(
                    pl.ds(pl.multiple_of(step * 16, 16), 16),
                    slice(low * 128, low * 128 + 128),
                    turned[low * 16 : low * 16 + 16],
                )

        loop(12, body)

    def from_matrix(first, rows):
        def body(step):
            at = pl.ds(pl.multiple_of(step * 16, 16), 16)
            parts = [acc[at, low * 128 : low * 128 + 128] for low in range(8)]
            turned = jnp.concatenate(parts, axis=0).T
            for b in range(3):
                flat[pl.ds(first + 3 * step + b, Q, stride=rows), :] = turned[b * 32 : b * 32 + 32]

        loop(12, body)

    def mate(d):
        return ((s // 2 + (d + 1) // 2) % 2) * 2 + (s % 2 + (d + 1) % 2) % 2

    def s_copy(phase, src, dst, d):
        to = mate(d)
        return pltpu.make_async_remote_copy(
            src_ref=src(to),
            dst_ref=dst.at[s],
            send_sem=s_send.at[phase, to],
            recv_sem=s_recv.at[phase, s],
            device_id={"row": y * 4 + to, "col": q},
            device_id_type=MESH,
        )

    def s_wait(phase, dst, frm):
        pltpu.make_async_remote_copy(
            src_ref=dst.at[frm],
            dst_ref=dst.at[frm],
            send_sem=s_send.at[phase, frm],
            recv_sem=s_recv.at[phase, frm],
            device_id={"row": y * 4 + frm, "col": q},
            device_id_type=MESH,
        ).wait_recv()

    def s_send_wait(phase, src, dst):
        loop(3, lambda d: s_copy(phase, src, dst, d).wait_send())

    def project(block):
        normed, inverse = normalize(pair_ref[block].astype(F32).T)
        rounded = normed.astype(BF16)
        xn[block] = normed
        xb[block] = rounded
        inv[block] = inverse
        p = nn(win_ref[...], rounded)
        proj[block] = p
        mask = mask_ref[block]
        values = (
            (mask * jax.nn.sigmoid(p[C : 2 * C]) * p[:C]).astype(BF16),
            (mask * jax.nn.sigmoid(p[3 * C : 4 * C]) * p[2 * C : 3 * C]).astype(BF16),
        )
        for array in range(2):
            for yy in range(Y):
                ys_a[yy, array * BLOCKS + block] = values[array][yy * 32 : yy * 32 + 32]

    loop(BLOCKS, project)
    pl.semaphore_wait(barrier, Q + R - 2)

    flat[72 * 32 :, :] = jnp.zeros((8 * 32, C), F32)
    y_exchange(0, ys_a, yr_a)
    spread(2, yr_a)
    z_exchange(0, zs_a, zr_a, PAIRED, pick(PAIRED))

    def write_to(ref, *index):
        def write(rows, columns, value):
            ref[(*index, rows, columns)] = value

        return write

    to_matrix(36, PAIRED, write_to(right, s))
    loop(3, lambda d: s_copy(0, lambda to: right.at[s], right, d).start())
    to_matrix(0, PAIRED, write_to(left, s))
    loop(3, lambda d: s_copy(1, lambda to: left.at[s], left, d).start())

    acc[...] = jnp.zeros_like(acc)

    def triangle(part):
        tri = nt(left[s], right[part]).astype(BF16)
        acc[...] += nt(tri, order_ref[part][:, :ROWS])

    triangle(s)

    def triangle_step(d):
        s_wait(0, right, mate(d))
        triangle(mate(d))

    loop(3, triangle_step)
    from_matrix(0, SINGLE)
    z_exchange(1, zs_t, zr_t, SINGLE, stored(SINGLE))
    gather_up(1, SINGLE, ys_t)
    y_exchange(1, ys_t, yr_t)

    gw5[...] = jnp.zeros_like(gw5)

    def tile(block):
        tri = jnp.concatenate([yr_t[yy, block] for yy in range(Y)], axis=0).astype(F32)
        normed, inverse = normalize(tri)
        rounded = normed.astype(BF16)
        linear = nn(wout_ref[...], rounded)
        gate = jax.nn.sigmoid(proj[block, 4 * C : 5 * C])
        upd_ref[block] = (gate * linear).T.astype(BF16)
        upstream = cot_ref[block].astype(F32).T
        grad_linear = (upstream * gate).astype(BF16)
        logit[block] = (upstream * linear * gate * (1.0 - gate)).astype(BF16)
        gw5[...] += nt(rounded, grad_linear)
        grad_tri = norm_backward(nn(woutb_ref[...], grad_linear), normed, inverse).astype(BF16)
        for yy in range(Y):
            ys_g[yy, block] = grad_tri[yy * 32 : yy * 32 + 32]

    loop(BLOCKS, tile)
    y_exchange(2, ys_g, yr_g)
    spread(1, yr_g)
    z_exchange(2, zs_g, zr_g, SINGLE, pick(SINGLE))
    to_matrix(0, SINGLE, write_to(gmat))

    def columns_of(part):
        gs[part] = nn(gmat[...], order_ref[part]).astype(BF16)

    loop(S, columns_of)
    loop(3, lambda d: s_copy(2, lambda to: gs.at[to], gr, d).start())
    gr[s] = gs[s]
    acc[...] = jnp.zeros_like(acc)

    def grad_left(part):
        acc[...] += nn(gs[part][:, :ROWS], right[part])

    loop(S, grad_left)
    from_matrix(0, PAIRED)
    acc[...] = jnp.zeros_like(acc)

    def grad_right(part):
        acc[...] += tn(gr[part][:, :ROWS], left[part])

    grad_right(s)

    def grad_right_step(d):
        s_wait(1, left, mate(d))
        s_wait(2, gr, mate(d))
        grad_right(mate(d))

    loop(3, grad_right_step)
    from_matrix(36, PAIRED)
    z_exchange(3, zs_b, zr_b, PAIRED, stored(PAIRED))
    gather_up(2, PAIRED, ys_b)
    y_exchange(3, ys_b, yr_b)

    gwin[...] = jnp.zeros_like(gwin)

    def finish(block):
        mask = mask_ref[block]
        grads = []
        for array in range(2):
            parts = [yr_b[yy, array * BLOCKS + block] for yy in range(Y)]
            upstream = jnp.concatenate(parts, axis=0).astype(F32) * mask
            value = proj[block, 2 * array * C : (2 * array + 1) * C]
            gate = jax.nn.sigmoid(proj[block, (2 * array + 1) * C : (2 * array + 2) * C])
            grads.append((upstream * gate).astype(BF16))
            grads.append((upstream * value * gate * (1.0 - gate)).astype(BF16))
        stack = jnp.concatenate(grads + [logit[block]], axis=0)
        grad = norm_backward(nn(wback_ref[...], stack), xn[block], inv[block])
        gpair_ref[block] = grad.T
        gwin[...] += nt(xb[block], stack)

    loop(BLOCKS, finish)

    for m in range(5):
        wfull[m * C : (m + 1) * C] = gwin[:, m * C : (m + 1) * C]
    wfull[5 * C :] = gw5[...]
    for part in range(R):
        ws1[part] = wfull[part * 48 : part * 48 + 48].astype(BF16)

    def other_row(d):
        return (r + 1 + d) % R

    def other_col(d):
        return (q + 1 + d) % Q

    def w1_copy(to, at):
        return pltpu.make_async_remote_copy(
            src_ref=ws1.at[to],
            dst_ref=wr1.at[at],
            send_sem=w1_send.at[to],
            recv_sem=w1_recv.at[at],
            device_id={"row": to, "col": q},
            device_id_type=MESH,
        )

    def w2_copy(to, at):
        return pltpu.make_async_remote_copy(
            src_ref=ws2,
            dst_ref=wr2.at[at],
            send_sem=w2_send.at[to],
            recv_sem=w2_recv.at[at],
            device_id={"row": r, "col": to},
            device_id_type=MESH,
        )

    def w3_copy(to, at):
        return pltpu.make_async_remote_copy(
            src_ref=ws3,
            dst_ref=wr3.at[at],
            send_sem=w3_send.at[to],
            recv_sem=w3_recv.at[at],
            device_id={"row": to, "col": q},
            device_id_type=MESH,
        )

    loop(R - 1, lambda d: w1_copy(other_row(d), r).start())
    wr1[r] = ws1[r]
    loop(R - 1, lambda d: w1_copy(other_row(d), other_row(d)).wait_recv())
    ws2[...] = sum(wr1[part].astype(F32) for part in range(R)).astype(BF16)
    loop(Q - 1, lambda d: w2_copy(partner(d), q).start())
    wr2[q] = ws2[...]
    loop(Q - 1, lambda d: w2_copy(other_col(d), other_col(d)).wait_recv())
    ws3[...] = sum(wr2[part].astype(F32) for part in range(Q)) * (1.0 / (R * 48))
    loop(R - 1, lambda d: w3_copy(other_row(d), r).start())
    wr3[r] = ws3[...]
    loop(R - 1, lambda d: w3_copy(other_row(d), other_row(d)).wait_recv())
    gw_ref[...] = wr3[...]

    for phase, (src, dst) in enumerate(((ys_a, yr_a), (ys_t, yr_t), (ys_g, yr_g), (ys_b, yr_b))):
        loop(Y - 1, lambda d, p=phase, a=src, b=dst: y_copy(p, a, b, d).wait_send())
    for phase, (src, dst) in enumerate(((zs_a, zr_a), (zs_t, zr_t), (zs_g, zr_g), (zs_b, zr_b))):
        loop(Q - 1, lambda d, p=phase, a=src, b=dst: z_copy(p, a, b, other_col(d)).wait_send())
    s_send_wait(0, lambda to: right.at[s], right)
    s_send_wait(1, lambda to: left.at[s], left)
    s_send_wait(2, lambda to: gs.at[to], gr)
    loop(R - 1, lambda d: w1_copy(other_row(d), r).wait_send())
    loop(Q - 1, lambda d: w2_copy(other_col(d), q).wait_send())
    loop(R - 1, lambda d: w3_copy(other_row(d), r).wait_send())


def on_device(pair, pair_mask, weights, cotangent):
    def blocks(values, tail):
        values = values.reshape((3, 16, 3, 8) + tail)
        return values.transpose((0, 2, 3, 1) + tuple(range(4, 4 + len(tail))))

    def tile(values):
        values = values.reshape(3, 3, 8, 16, C).transpose(0, 3, 1, 2, 4)
        return values.reshape(48, 24, C)

    pair_in = blocks(pair, (C,)).reshape(BLOCKS, C, C)
    cot_in = blocks(cotangent, (C,)).reshape(BLOCKS, C, C)
    mask_in = blocks(pair_mask.astype(F32), ()).reshape(BLOCKS, 1, C)
    win = weights[:5].transpose(0, 2, 1).reshape(5 * C, C)
    wback = weights[:5].transpose(1, 0, 2).reshape(C, 5 * C)
    vmem = pl.BlockSpec(memory_space=pltpu.VMEM)

    def y_pair(arrays):
        return [pltpu.VMEM((Y, arrays * BLOCKS, 32, C), BF16)] * 2

    def z_pair(rows):
        return [pltpu.VMEM((Q, rows, C), BF16)] * 2

    def sems(*shape):
        return [pltpu.SemaphoreType.DMA(shape)] * 2

    update, grad_pair, grad_weights = pl.pallas_call(
        kernel,
        out_shape=(
            jax.ShapeDtypeStruct((BLOCKS, C, C), BF16),
            jax.ShapeDtypeStruct((BLOCKS, C, C), F32),
            jax.ShapeDtypeStruct((R, 48, C), F32),
        ),
        in_specs=[vmem] * 8,
        out_specs=(vmem, vmem, vmem),
        scratch_shapes=[
            pltpu.VMEM((BLOCKS, 5 * C, C), F32),
            pltpu.VMEM((BLOCKS, C, C), F32),
            pltpu.VMEM((BLOCKS, C, C), BF16),
            pltpu.VMEM((BLOCKS, 1, C), F32),
            pltpu.VMEM((BLOCKS, C, C), BF16),
            pltpu.VMEM((Q * PAIRED, C), F32),
            *y_pair(2),
            *z_pair(PAIRED),
            *y_pair(1),
            *z_pair(SINGLE),
            *y_pair(1),
            *z_pair(SINGLE),
            *y_pair(2),
            *z_pair(PAIRED),
            pltpu.VMEM((S, ROWS, WIDE), BF16),
            pltpu.VMEM((S, ROWS, WIDE), BF16),
            pltpu.VMEM((ROWS, WIDE), BF16),
            pltpu.VMEM((ROWS, WIDE), F32),
            pltpu.VMEM((S, ROWS, 256), BF16),
            pltpu.VMEM((S, ROWS, 256), BF16),
            pltpu.VMEM((C, C), F32),
            pltpu.VMEM((C, 5 * C), F32),
            pltpu.VMEM((6 * C, C), F32),
            pltpu.VMEM((R, 48, C), BF16),
            pltpu.VMEM((R, 48, C), BF16),
            pltpu.VMEM((48, C), BF16),
            pltpu.VMEM((Q, 48, C), BF16),
            pltpu.VMEM((48, C), F32),
            pltpu.VMEM((R, 48, C), F32),
            *sems(4, Y),
            *sems(4, Q),
            *sems(3, S),
            *sems(R),
            *sems(Q),
            *sems(R),
        ],
        compiler_params=pltpu.CompilerParams(
            collective_id=0, has_side_effects=True, vmem_limit_bytes=56 * 1024 * 1024
        ),
    )(pair_in, cot_in, mask_in, win, wback, weights[5].T, weights[5], jnp.asarray(column_order()))
    return tile(update), tile(grad_pair), grad_weights.reshape(6, C, C)


def solution(mesh):
    placed = (P("row", "col", None), P("row", "col"), P(), P("row", "col", None))
    return jax.shard_map(
        on_device,
        mesh=mesh,
        in_specs=placed,
        out_specs=(P("row", "col", None), P("row", "col", None), P()),
        check_vma=False,
    )
```

time: 834 us -> 248 us (0.30)
  waiting for transfers between devices: 538 us -> 0 us
  Pallas kernels: 0 us -> 234 us
  blocking collectives: 132 us -> 0 us
  local copies, waits for them, and re-layouts: 83.4 us -> 12.8 us
  matrix products: 25.7 us -> 0 us
  starting transfers between devices: 21.5 us -> 0 us
  other arithmetic: 16.6 us -> 0.75 us
  between operations: 14.1 us -> 0.67 us
    psum x1 -> x0, waiting for transfers between devices: 456 us -> none  [on_device(): lax.psum((input_terms, output_terms), ('row', 'col'))]
    pallas_call x0 -> x1, Pallas kernels: none -> 234 us  [on_device(): pl.pallas_call(kernel, out_shape=(jax.ShapeDtypeStruct((BLOCKS, C, C), BF...]
    all_to_all x4 -> x0, blocking collectives: 132 us -> none  [the longest x1 41 us: on_device(): lax.all_to_all(right_act.transpose(2, 0, 1), 'col', split_axis=0, concat_...]
    all_gather x3 -> x0, waiting for transfers between devices: 74.2 us -> none  [the longest x1 46.9 us: on_device(): left_piece = lax.all_gather(left_chan, 'row', axis=1, tiled=True)]
    unnamed x51 -> x6, local copies, waits for them, and re-layouts: 41.7 us -> 1.94 us
    dot_general x9 -> x0, matrix products: 25.7 us -> none  [the longest x1 4.27 us: on_device(): jnp.einsum('cij,cjk->cik', grad_chan, right_full, preferred_element_type=...]
    all_to_all x2 -> x0, starting transfers between devices: 21.4 us -> none  [the longest x1 14.6 us: on_device(): lax.all_to_all(right_grad_chan, 'col', split_axis=2, concat_axis=0, tiled...]
    convert_element_type x11 -> x0, local copies, waits for them, and re-layouts: 18.2 us -> none  [the longest x2 3.24 us: on_device(): tri_tile.transpose(1, 2, 0).astype(jnp.float32)]
  transfers between devices with their start and end apart: 6 -> 0, of which waited for: 5 -> 0; matrix products, arithmetic and copies ran while one was open for 6% -> 0% of each run, Pallas kernels for 0% -> 0%
where the time goes in v1:
time: 248 us
  Pallas kernels  234 us (94%)
  local copies, waits for them, and re-layouts  12.8 us (5%)
    pallas_call x1, Pallas kernels, on_device(): pl.pallas_call(kernel, out_shape=(jax.ShapeDtypeStruct((BLOCKS, C, C), BF...  234 us

profile of v1, /device:TPU:1, one launch (start us, length us, event | category | flops | bytes accessed | tf_op | source)
XLA Modules:
  0.0 247.9 jit_solution(1777082037422430708)
XLA Ops:
  0.6 0.0 copy-start.1
  0.6 0.8 convert_element_type.3
  1.4 0.1 reshape.49
  1.5 0.7 reshape.50.mask_ref
  2.2 1.4 slice_bitcast_fusion.1
  3.5 0.7 copy.21.wout_ref
  4.3 0.9 slice.8
  5.2 0.2 copy.24
  5.4 0.0 copy-start
  5.4 0.8 copy.20.wback_ref
  6.2 1.7 copy.16
  7.9 0.0 copy-done.1
  7.9 0.8 copy.17
  8.7 0.0 copy-done
  8.7 233.6 %shard_map.76 = (bf16[9,128,128]{2,1,0:T(8,128)(2,1)}, f32[9,128,128]{2,1,0:T(8,128)}, f32[16,48,128]{2,1,0:T(8,128)}) custom-call(bf16[9,128,128]{2,1,0:T(8,128)(2,1)} %bitcast.35, bf16[9,128,128]{2,1,0:T(8,128)(2,1)} %bitcast.36, f32[9,1,128]{2,1,0:T(1,128)} %reshape.50.mask_ref, bf16[640,128]{1,0:T(8,128)(2,1)} %bitcast.34, ...), custom_call_target="tpu_custom_call" | custom-call | tf_op jit(solution)/shard_map/pallas_call | solution.py:506
  242.3 1.8 copy.22
  244.0 2.1 copy.23
  246.1 1.8 copy.26
  (1 shorter events, 0.0 us)
Async XLA Ops:
  0.6 7.3 %copy-start.1 = (bf16[48,24,128]{2,1,0:T(8,128)(2,1)S(1)}, bf16[48,24,128]{2,1,0:T(8,128)(2,1)}, u32[]{:S(2)}) copy-start(bf16[48,24,128]{2,1,0:T(8,128)(2,1)} %param.8) | copy-start | bytes 884740
  5.4 3.3 %copy-start = (bf16[5,128,128]{1,2,0:T(8,128)(2,1)}, bf16[5,128,128]{1,2,0:T(8,128)(2,1)S(1)}, u32[]{:S(2)}) copy-start(bf16[5,128,128]{1,2,0:T(8,128)(2,1)S(1)} %copy.24) | copy-start | bytes 491524

commit v2 on v0

v2 whole, which is shorter than its diff:
```python
import jax
import jax.numpy as jnp
import numpy as np
from jax import lax
from jax.experimental import pallas as pl
from jax.experimental.pallas import tpu as pltpu
from jax.sharding import PartitionSpec as P


F32 = jnp.float32
BF16 = jnp.bfloat16
C = 128
BLOCKS = 9
Y, S, Z, G = 4, 4, 16, 8
ROWS = 192
WIDE = 1024
TILE_ROWS = 384
MESH = pl.DeviceIdType.MESH
RIGHT, LEFT, TRI0, TRI1, GRAD0, GRAD1, BACK_L, BACK_R = range(8)
PHASES = ((9, 80), (9, 80), (3, 32), (6, 48), (3, 32), (6, 48), (9, 80), (9, 80))
PARTS = ((0, 1), (1, 2))


def nt(a, b):
    return lax.dot_general(a, b, (((1,), (1,)), ((), ())), preferred_element_type=F32)


def nn(a, b):
    return lax.dot_general(a, b, (((1,), (0,)), ((), ())), preferred_element_type=F32)


def normalize(values):
    average = jnp.mean(values, axis=0, keepdims=True)
    centred = values - average
    variance = jnp.mean(centred * centred, axis=0, keepdims=True)
    inverse = lax.rsqrt(variance + 1e-05)
    return centred * inverse, inverse


def norm_backward(upstream, normed, inverse):
    first = jnp.mean(upstream, axis=0, keepdims=True)
    second = jnp.mean(upstream * normed, axis=0, keepdims=True)
    return inverse * (upstream - first - normed * second)


def column_order():
    low, block, tile = np.meshgrid(np.arange(8), np.arange(3), np.arange(32), indexing="ij")
    residue = (tile * 24 + block * 8 + low).reshape(-1)
    place = (low * 128 + block * 32 + tile).reshape(-1)
    y, s, inner = residue // 192, residue // 48 % 4, residue % 48
    order = np.zeros((S, ROWS, WIDE), np.float32)
    order[s, y * 48 + inner, place] = 1
    return order.astype(jnp.bfloat16)


def loop(count, body):
    def step(i, carry):
        body(i)
        return carry

    lax.fori_loop(0, count, step, 0)


def at(start, size, unit=8):
    return pl.ds(pl.multiple_of(start * unit, unit), size)


def kernel(
    pair_hbm,
    cot_hbm,
    order_hbm,
    mask_ref,
    weights_ref,
    upd_hbm,
    gpair_hbm,
    gw_ref,
    pair_v,
    cot_v,
    order,
    upd_v,
    gpair_v,
    wt,
    wback,
    proj,
    xn,
    xb,
    inv,
    stack,
    flat,
    turned,
    left,
    right,
    gmat,
    tri,
    gs,
    gts,
    gtr,
    gwin,
    *rest,
):
    rest = list(rest)
    ys, yr, zs, zr = ([rest.pop(0) for _ in PHASES] for _ in range(4))
    sums = [[rest.pop(0) for _ in range(9)] for _ in range(2)]
    y_send, y_recv, z_send, z_recv, s_send, s_recv = (rest.pop(0) for _ in range(6))
    w_sems = [[rest.pop(0) for _ in range(10)] for _ in range(2)]
    local = rest.pop(0)

    r = lax.axis_index("row")
    q = lax.axis_index("col")
    y, s = r // 4, r % 4
    half, z = q // 16, q % 16
    g = y * 2 + half

    def group(other):
        return {"row": (other // 2) * 4 + s, "col": (other % 2) * 16 + z}

    def along(other):
        return {"row": r, "col": half * 16 + other}

    def mate(d):
        return ((s // 2 + (d + 1) // 2) % 2) * 2 + (s % 2 + (d + 1) % 2) % 2

    def shared(other):
        return {"row": y * 4 + other, "col": q}

    def next_g(d):
        return (g + 1 + d) % G

    def next_z(step):
        t = Z - 1 - step
        hop = ((t + 1) // 2) * (2 * (t % 2) - 1)
        return (z + hop + Z) % Z

    barrier = pltpu.get_barrier_semaphore()

    def greet(device):
        pl.semaphore_signal(barrier, inc=1, device_id=device, device_id_type=MESH)

    loop(Z - 1, lambda d: greet(along(next_z(d))))
    loop(G - 1, lambda d: greet(group(next_g(d))))
    loop(S - 1, lambda d: greet(shared(mate(d))))

    load_pair = pltpu.make_async_copy(pair_hbm, pair_v, local.at[0])
    load_cot = pltpu.make_async_copy(cot_hbm, cot_v, local.at[1])
    load_order = pltpu.make_async_copy(order_hbm, order, local.at[2])
    load_pair.start()
    load_cot.start()
    load_order.start()

    def y_copy(phase, to, slot):
        return pltpu.make_async_remote_copy(
            src_ref=ys[phase].at[to],
            dst_ref=yr[phase].at[slot],
            send_sem=y_send.at[phase, to],
            recv_sem=y_recv.at[phase, slot],
            device_id=group(to),
            device_id_type=MESH,
        )

    def y_start(phase):
        loop(G - 1, lambda d: y_copy(phase, next_g(d), g).start())
        yr[phase][g] = ys[phase][g]

    def y_wait(phase):
        loop(G - 1, lambda d: y_copy(phase, next_g(d), next_g(d)).wait_recv())

    def z_copy(phase, to, slot):
        return pltpu.make_async_remote_copy(
            src_ref=zs[phase].at[to],
            dst_ref=zr[phase].at[slot],
            send_sem=z_send.at[phase, to],
            recv_sem=z_recv.at[phase, slot],
            device_id=along(to),
            device_id_type=MESH,
        )

    def z_start(phase, make):
        def send(step):
            to = next_z(step)
            zs[phase][to] = make(to)
            z_copy(phase, to, z).start()

        loop(Z - 1, send)
        zr[phase][z] = make(z)

    def z_wait(phase):
        rows = PHASES[phase][1]

        def receive(step):
            frm = next_z(Z - 2 - step)
            z_copy(phase, frm, frm).wait_recv()
            flat[at(frm * (rows // 16), rows, 16), :] = zr[phase][frm].astype(F32)

        flat[at(z * (rows // 16), rows, 16), :] = zr[phase][z].astype(F32)
        loop(Z - 1, receive)

    def z_start_up(phase):
        blocks, rows = PHASES[phase]

        def spread(step):
            flat[at(step, 16, 16), :] = yr[phase][step // blocks, step % blocks].astype(F32)

        loop(G * blocks, spread)
        z_start(phase, lambda to: flat[pl.ds(to, rows, stride=Z), :].astype(BF16))

    def z_start_back(phase):
        rows = PHASES[phase][1]
        z_start(phase, lambda to: flat[at(to * (rows // 16), rows, 16), :].astype(BF16))

    def y_start_back(phase):
        blocks, rows = PHASES[phase]

        def body(step):
            ys[phase][step // blocks, step % blocks] = flat[pl.ds(step, Z, stride=rows), :].astype(BF16)

        loop(G * blocks, body)
        y_start(phase)

    def split(part):
        first, count = part
        return lambda step: (step // count, first + step % count, step % count)

    def turn_up(phase, part):
        blocks, rows = PHASES[phase]

        def body(step):
            yy, row, own = split(part)(step)
            pieces = [
                flat[pl.ds((yy * 2 + hh) * blocks + own * 3 + b, Z, stride=rows), :]
                for b in range(3)
                for hh in range(2)
            ]
            pieces.append(jnp.zeros((32, C), F32))
            turned[at(yy * 3 + row, C, C), :] = jnp.concatenate(pieces, axis=0).T

        loop(Y * part[1], body)

    def turn_back(phase, part):
        blocks, rows = PHASES[phase]

        def body(step):
            yy, row, own = split(part)(step)
            values = turned[at(yy * 3 + row, C, C), :].T
            for b in range(3):
                for hh in range(2):
                    first = b * 32 + hh * 16
                    flat[pl.ds((yy * 2 + hh) * blocks + own * 3 + b, Z, stride=rows), :] = values[
                        first : first + 16
                    ]

        loop(Y * part[1], body)

    def low_columns(low):
        return at(low, C, C)

    def matrix(write):
        def body(low):
            write(low_columns(low), turned[pl.ds(low, ROWS, stride=8), :].astype(BF16))

        loop(8, body)

    def from_matrix(make):
        def body(low):
            turned[pl.ds(low, ROWS, stride=8), :] = make(low_columns(low))

        loop(8, body)

    def s_copy(phase, src, dst, slot, to):
        return pltpu.make_async_remote_copy(
            src_ref=src,
            dst_ref=dst,
            send_sem=s_send.at[phase, to],
            recv_sem=s_recv.at[phase, slot],
            device_id=shared(to),
            device_id_type=MESH,
        )

    def share(phase, ref):
        s_copy(phase, ref.at[s], ref.at[s], s, mate(1)).start()
        s_copy(phase, ref.at[s], ref.at[s], s, mate(0)).start()

    def passing_on(phase, ref):
        return pltpu.make_async_remote_copy(
            src_ref=ref.at[mate(1)],
            dst_ref=ref.at[mate(1)],
            send_sem=s_send.at[phase, mate(2)],
            recv_sem=s_recv.at[phase, mate(1)],
            device_id=shared(mate(0)),
            device_id_type=MESH,
        )

    def s_wait(phase, ref, slot):
        s_copy(phase, ref.at[slot], ref.at[slot], slot, slot).wait_recv()

    def pass_on(phase, ref):
        s_wait(phase, ref, mate(1))
        passing_on(phase, ref).start()

    def summing(which, rows):
        a_s, a_r, b_s, b_r, c_s, c_r, d_s, d_r, e_r = sums[which]
        sems = w_sems[which]

        def copy(step, src, dst, to, slot, device):
            return pltpu.make_async_remote_copy(
                src_ref=src,
                dst_ref=dst,
                send_sem=sems[2 * step].at[to],
                recv_sem=sems[2 * step + 1].at[slot],
                device_id=device,
                device_id_type=MESH,
            )

        copies = (
            lambda to, slot: copy(0, a_s.at[to], a_r.at[slot], to, slot, group(to)),
            lambda to, slot: copy(1, b_s.at[to], b_r.at[slot], to, slot, shared(to)),
            lambda to, slot: copy(2, c_s, c_r.at[slot], to, slot, along(to)),
            lambda to, slot: copy(3, d_s, d_r.at[slot], to, slot, shared(to)),
            lambda to, slot: copy(4, d_r, e_r.at[slot], to, slot, group(to)),
        )
        others = ((G - 1, next_g), (S - 1, mate), (Z - 1, next_z), (S - 1, mate), (G - 1, next_g))
        mine = (g, s, z, s, g)

        def start(step):
            count, other = others[step]
            loop(count, lambda d: copies[step](other(d), mine[step]).start())

        def wait(step):
            count, other = others[step]
            loop(count, lambda d: copies[step](other(d), other(d)).wait_recv())

        def first():
            start(0)
            a_r[g] = a_s[g]

        def second():
            wait(0)
            total = sum(a_r[k].astype(F32) for k in range(G))
            for k in range(S):
                b_s[k] = total[k * (rows // S) : (k + 1) * (rows // S)]
            start(1)
            b_r[s] = b_s[s]

        def third():
            wait(1)
            c_s[...] = sum(b_r[k] for k in range(S))
            start(2)
            c_r[z] = c_s[...]

        def fourth():
            wait(2)
            d_s[...] = sum(c_r[k] for k in range(Z)) * (1.0 / 768.0)
            start(3)
            d_r[s] = d_s[...]

        def fifth():
            wait(3)
            start(4)
            e_r[g] = d_r[...]

        def last(write):
            wait(4)
            for k in range(G):
                write(k, e_r[k].reshape(rows, C))

        def sent():
            for step, (count, other) in enumerate(others):
                loop(count, lambda d, c=copies[step], o=other: c(o(d), o(d)).wait_send())

        return first, second, third, fourth, fifth, last, sent

    for m in range(6):
        wt[m * C : (m + 1) * C] = weights_ref[m].astype(F32).T.astype(BF16)
    for m in range(5):
        wback[:, m * C : (m + 1) * C] = weights_ref[m]
    gwin[...] = jnp.zeros_like(gwin)

    def tile_rows(ref, row):
        return ref[at(row, TILE_ROWS, TILE_ROWS), :].astype(F32).reshape(16, 24, C)

    def block_of(values, b):
        return values[:, b * 8 : b * 8 + 8, :].reshape(C, C).T

    def rows_of(blocks):
        return jnp.concatenate([b.T.reshape(16, 8, C) for b in blocks], axis=1).reshape(TILE_ROWS, C)

    load_pair.wait()

    def project(row):
        values = tile_rows(pair_v, row)
        for b in range(3):
            block = row * 3 + b
            normed, inverse = normalize(block_of(values, b))
            rounded = normed.astype(BF16)
            xn[block] = normed
            xb[block] = rounded
            inv[block] = inverse
            p = nn(wt[: 5 * C], rounded)
            proj[block] = p
            mask = mask_ref[block]
            left_act = (mask * jax.nn.sigmoid(p[C : 2 * C]) * p[:C]).astype(BF16)
            right_act = (mask * jax.nn.sigmoid(p[3 * C : 4 * C]) * p[2 * C : 3 * C]).astype(BF16)
            for k in range(G):
                ys[LEFT][k, block] = left_act[k * 16 : k * 16 + 16]
                ys[RIGHT][k, block] = right_act[k * 16 : k * 16 + 16]

    loop(3, project)
    pl.semaphore_wait(barrier, Z + G + S - 3)

    whole = (0, 3)
    y_start(RIGHT)
    y_wait(RIGHT)
    y_start(LEFT)
    flat[G * BLOCKS * Z :, :] = jnp.zeros((8 * Z, C), F32)
    z_start_up(RIGHT)
    y_wait(LEFT)
    z_start_up(LEFT)

    def write_to(ref, *index):
        def write(columns, value):
            ref[(*index, slice(None), columns)] = value

        return write

    z_wait(RIGHT)
    turn_up(RIGHT, whole)
    matrix(write_to(right, s))
    share(0, right)
    load_cot.wait()
    load_order.wait()
    pass_on(0, right)
    z_wait(LEFT)
    turn_up(LEFT, whole)
    matrix(write_to(left, s))

    def triangle(part):
        tri[part, :, :ROWS] = nt(left[s], right[part]).astype(BF16)

    triangle(s)
    triangle(mate(1))
    s_wait(0, right, mate(0))
    triangle(mate(0))
    s_wait(0, right, mate(2))
    triangle(mate(2))
    from_matrix(
        lambda columns: sum(nn(tri[k, :, :ROWS], order[k, :, columns]) for k in range(S))
    )
    for part, phase in enumerate((TRI0, TRI1)):
        turn_back(phase, PARTS[part])
        z_start_back(phase)
    share(1, left)

    def tile(phase, back, part):
        def body(step):
            row = part[0] + step
            cotangent = tile_rows(cot_v, row)
            updates = []
            for b in range(3):
                block, own = row * 3 + b, step * 3 + b
                values = jnp.concatenate([yr[phase][k, own] for k in range(G)], axis=0)
                normed, inverse = normalize(values.astype(F32))
                rounded = normed.astype(BF16)
                linear = nn(wt[5 * C :], rounded)
                gate = jax.nn.sigmoid(proj[block, 4 * C :])
                updates.append(gate * linear)
                upstream = block_of(cotangent, b)
                grad_linear = (upstream * gate).astype(BF16)
                logit = (upstream * linear * gate * (1.0 - gate)).astype(BF16)
                stack[block, 4 * C :] = logit
                gwin[:, 4 * C : 5 * C] += nt(xb[block], logit)
                gwin[:, 5 * C :] += nt(rounded, grad_linear)
                grad_xout = nn(weights_ref[5], grad_linear)
                grad = norm_backward(grad_xout, normed, inverse).astype(BF16)
                for k in range(G):
                    ys[back][k, own] = grad[k * 16 : k * 16 + 16]
            upd_v[at(row, TILE_ROWS, TILE_ROWS), :] = rows_of(updates).astype(BF16)

        loop(part[1], body)

    z_wait(TRI0)
    y_start_back(TRI0)
    y_wait(TRI0)
    tile(TRI0, GRAD0, PARTS[0])
    y_start(GRAD0)
    z_wait(TRI1)
    y_start_back(TRI1)
    y_wait(GRAD0)
    z_start_up(GRAD0)
    y_wait(TRI1)
    tile(TRI1, GRAD1, PARTS[1])
    y_start(GRAD1)
    store_upd = pltpu.make_async_copy(upd_v, upd_hbm, local.at[0])
    store_upd.start()
    early = summing(0, 32)
    for k in range(G):
        m, first = 4 + k // 4, (k % 4) * 32
        sums[0][0][k] = gwin[first : first + 32, m * C : (m + 1) * C].astype(BF16)
    y_wait(GRAD1)
    z_start_up(GRAD1)
    early[0]()
    pass_on(1, left)
    z_wait(GRAD0)
    turn_up(GRAD0, PARTS[0])
    early[1]()
    z_wait(GRAD1)
    turn_up(GRAD1, PARTS[1])
    matrix(write_to(gmat))

    def columns_of(part):
        gts[part, :, :ROWS] = nt(order[part], gmat[...]).astype(BF16)

    loop(S, columns_of)

    def give(d):
        return s_copy(2, gts.at[mate(d)], gtr.at[s], s, mate(d))

    loop(S - 1, lambda d: give(d).start())
    gtr[s] = gts[s]

    def rows_for(part):
        gs[part, :, :ROWS] = nt(gmat[...], order[part]).astype(BF16)

    loop(S, rows_for)
    from_matrix(
        lambda columns: sum(nn(gs[k, :, :ROWS], right[k, :, columns]) for k in range(S))
    )
    turn_back(BACK_L, whole)
    z_start_back(BACK_L)
    early[2]()
    s_wait(1, left, mate(0))
    s_wait(1, left, mate(2))
    loop(S - 1, lambda d: s_wait(2, gtr, mate(d)))
    from_matrix(
        lambda columns: sum(nn(gtr[k, :, :ROWS], left[k, :, columns]) for k in range(S))
    )
    turn_back(BACK_R, whole)
    z_start_back(BACK_R)
    early[3]()

    def grads_of(phase, array):
        def body(block):
            values = jnp.concatenate([yr[phase][k, block] for k in range(G)], axis=0)
            upstream = values.astype(F32) * mask_ref[block]
            first = 2 * array * C
            value = proj[block, first : first + C]
            gate = jax.nn.sigmoid(proj[block, first + C : first + 2 * C])
            pieces = (upstream * gate, upstream * value * gate * (1.0 - gate))
            for k in range(2):
                piece = pieces[k].astype(BF16)
                columns = slice(first + k * C, first + (k + 1) * C)
                stack[block, columns] = piece
                gwin[:, columns] += nt(xb[block], piece)

        loop(BLOCKS, body)

    z_wait(BACK_L)
    y_start_back(BACK_L)
    early[4]()
    y_wait(BACK_L)
    grads_of(BACK_L, 0)

    def write_early(k, rows):
        gw_ref[4 + k // 4, (k % 4) * 32 : (k % 4) * 32 + 32] = rows

    early[5](write_early)
    z_wait(BACK_R)
    y_start_back(BACK_R)
    y_wait(BACK_R)
    grads_of(BACK_R, 1)
    late = summing(1, 64)
    for k in range(G):
        m, first = k // 2, (k % 2) * 64
        sums[1][0][k] = gwin[first : first + 64, m * C : (m + 1) * C].astype(BF16)
    late[0]()

    def store_gpair(row):
        rows = at(row, TILE_ROWS, TILE_ROWS)
        return pltpu.make_async_copy(gpair_v.at[rows], gpair_hbm.at[rows], local.at[3 + row])

    def finish(row):
        grads = []
        for b in range(3):
            block = row * 3 + b
            grads.append(norm_backward(nn(wback[...], stack[block]), xn[block], inv[block]))
        gpair_v[at(row, TILE_ROWS, TILE_ROWS), :] = rows_of(grads)
        store_gpair(row).start()

    loop(3, finish)
    for step in range(1, 5):
        late[step]()

    def write_late(k, rows):
        gw_ref[k // 2, (k % 2) * 64 : (k % 2) * 64 + 64] = rows

    late[5](write_late)

    store_upd.wait()
    loop(3, lambda row: store_gpair(row).wait())
    for phase in range(len(PHASES)):
        loop(G - 1, lambda d, p=phase: y_copy(p, next_g(d), g).wait_send())
        loop(Z - 1, lambda d, p=phase: z_copy(p, next_z(d), z).wait_send())
    for phase, ref in enumerate((right, left)):
        for d in range(2):
            s_copy(phase, ref.at[s], ref.at[s], s, mate(d)).wait_send()
        passing_on(phase, ref).wait_send()
    loop(S - 1, lambda d: give(d).wait_send())
    early[6]()
    late[6]()


def on_device(pair, pair_mask, weights, cotangent):
    pixels = pair.shape[0] * pair.shape[1]
    mask = pair_mask.astype(F32).reshape(3, 16, 3, 8).transpose(0, 2, 1, 3).reshape(BLOCKS, 1, C)
    vmem = pl.BlockSpec(memory_space=pltpu.VMEM)
    anywhere = pl.BlockSpec(memory_space=pl.ANY)

    def sems(*shape):
        return [pltpu.SemaphoreType.DMA(shape)] * 2

    def sum_buffers(rows):
        small = rows // S
        return [
            *[pltpu.VMEM((G, rows, C), BF16)] * 2,
            *[pltpu.VMEM((S, small, C), F32)] * 2,
            pltpu.VMEM((small, C), F32),
            pltpu.VMEM((Z, small, C), F32),
            pltpu.VMEM((small, C), F32),
            pltpu.VMEM((S, small, C), F32),
            pltpu.VMEM((G, S, small, C), F32),
        ]

    y_buffers = [pltpu.VMEM((G, blocks, 16, C), BF16) for blocks, _ in PHASES]
    z_buffers = [pltpu.VMEM((Z, rows, C), BF16) for _, rows in PHASES]
    update, grad_pair, grad_weights = pl.pallas_call(
        kernel,
        out_shape=(
            jax.ShapeDtypeStruct((pixels, C), BF16),
            jax.ShapeDtypeStruct((pixels, C), F32),
            jax.ShapeDtypeStruct((6, C, C), F32),
        ),
        in_specs=[anywhere] * 3 + [vmem] * 2,
        out_specs=(anywhere, anywhere, vmem),
        scratch_shapes=[
            pltpu.VMEM((pixels, C), BF16),
            pltpu.VMEM((pixels, C), BF16),
            pltpu.VMEM((S, ROWS, WIDE), BF16),
            pltpu.VMEM((pixels, C), BF16),
            pltpu.VMEM((pixels, C), F32),
            pltpu.VMEM((6 * C, C), BF16),
            pltpu.VMEM((C, 5 * C), BF16),
            pltpu.VMEM((BLOCKS, 5 * C, C), F32),
            pltpu.VMEM((BLOCKS, C, C), F32),
            pltpu.VMEM((BLOCKS, C, C), BF16),
            pltpu.VMEM((BLOCKS, 1, C), F32),
            pltpu.VMEM((BLOCKS, 5 * C, C), BF16),
            pltpu.VMEM((Z * 80, C), F32),
            pltpu.VMEM((12 * C, C), F32),
            pltpu.VMEM((S, ROWS, WIDE), BF16),
            pltpu.VMEM((S, ROWS, WIDE), BF16),
            pltpu.VMEM((ROWS, WIDE), BF16),
            *[pltpu.VMEM((S, ROWS, 256), BF16)] * 4,
            pltpu.VMEM((C, 6 * C), F32),
            *y_buffers,
            *y_buffers,
            *z_buffers,
            *z_buffers,
            *sum_buffers(32),
            *sum_buffers(64),
            *sems(len(PHASES), G),
            *sems(len(PHASES), Z),
            *sems(3, S),
            *[sem for _ in range(2) for n in (G, S, Z, S, G) for sem in sems(n)],
            pltpu.SemaphoreType.DMA((6,)),
        ],
        compiler_params=pltpu.CompilerParams(
            collective_id=0, has_side_effects=True, vmem_limit_bytes=56 * 1024 * 1024
        ),
    )(
        pair.reshape(pixels, C),
        cotangent.reshape(pixels, C),
        jnp.asarray(column_order()),
        mask,
        weights,
    )
    return update.reshape(pair.shape), grad_pair.reshape(pair.shape), grad_weights


def solution(mesh):
    placed = (P("row", "col", None), P("row", "col"), P(), P("row", "col", None))
    return jax.shard_map(
        on_device,
        mesh=mesh,
        in_specs=placed,
        out_specs=(P("row", "col", None), P("row", "col", None), P()),
        check_vma=False,
    )
```

time: 834 us -> 190 us (0.23)
  waiting for transfers between devices: 538 us -> 0 us
  Pallas kernels: 0 us -> 183 us
  blocking collectives: 132 us -> 0 us
  local copies, waits for them, and re-layouts: 83.4 us -> 5.3 us
  matrix products: 25.7 us -> 0 us
  starting transfers between devices: 21.5 us -> 0 us
  other arithmetic: 16.6 us -> 0.71 us
  between operations: 14.1 us -> 0.66 us
    psum x1 -> x0, waiting for transfers between devices: 456 us -> none  [on_device(): lax.psum((input_terms, output_terms), ('row', 'col'))]
    pallas_call x0 -> x1, Pallas kernels: none -> 183 us  [on_device(): pl.pallas_call(kernel, out_shape=(jax.ShapeDtypeStruct((pixels, C), BF16)...]
    all_to_all x4 -> x0, blocking collectives: 132 us -> none  [the longest x1 41 us: on_device(): lax.all_to_all(right_act.transpose(2, 0, 1), 'col', split_axis=0, concat_...]
    all_gather x3 -> x0, waiting for transfers between devices: 74.2 us -> none  [the longest x1 46.9 us: on_device(): left_piece = lax.all_gather(left_chan, 'row', axis=1, tiled=True)]
    unnamed x51 -> x5, local copies, waits for them, and re-layouts: 41.7 us -> 4.42 us
    dot_general x9 -> x0, matrix products: 25.7 us -> none  [the longest x1 4.27 us: on_device(): jnp.einsum('cij,cjk->cik', grad_chan, right_full, preferred_element_type=...]
    all_to_all x2 -> x0, starting transfers between devices: 21.4 us -> none  [the longest x1 14.6 us: on_device(): lax.all_to_all(right_grad_chan, 'col', split_axis=2, concat_axis=0, tiled...]
    convert_element_type x11 -> x0, local copies, waits for them, and re-layouts: 18.2 us -> none  [the longest x2 3.24 us: on_device(): tri_tile.transpose(1, 2, 0).astype(jnp.float32)]
  transfers between devices with their start and end apart: 6 -> 0, of which waited for: 5 -> 0; matrix products, arithmetic and copies ran while one was open for 6% -> 0% of each run, Pallas kernels for 0% -> 0%
where the time goes in v2:
time: 190 us
  Pallas kernels  183 us (96%)
  local copies, waits for them, and re-layouts  5.3 us (3%)
    pallas_call x1, Pallas kernels, on_device(): pl.pallas_call(kernel, out_shape=(jax.ShapeDtypeStruct((pixels, C), BF16)...  183 us
    unnamed x5, local copies, waits for them, and re-layouts  4.42 us

profile of v2, /device:TPU:1, one launch (start us, length us, event | category | flops | bytes accessed | tf_op | source)
XLA Modules:
  0.0 189.8 jit_solution(18089259995663521541)
XLA Ops:
  0.6 0.7 convert_element_type.3
  1.3 0.1 reshape.26
  1.4 0.1 copy.9
  1.5 0.7 reshape.30.mask_ref
  2.2 183.1 %shard_map.76 = (bf16[1152,128]{1,0:T(8,128)(2,1)}, f32[1152,128]{1,0:T(8,128)}, f32[6,128,128]{2,1,0:T(8,128)}) custom-call(bf16[1152,128]{1,0:T(8,128)(2,1)} %bitcast.11, bf16[1152,128]{1,0:T(8,128)(2,1)} %bitcast.12, bf16[4,192,1024]{2,1,0:T(8,128)(2,1)} %constant.2.clone.order_hbm, f32[9,1,128]{2,1,0:T(1,128)} %reshape.30.mask_ref, ...), custom_call_target="tpu_custom_call" | custom-call | tf_op jit(solution)/shard_map/pallas_call | solution.py:633
  185.4 0.0 copy-start
  185.4 1.8 copy.14
  187.1 1.9 %copy.15 = f32[48,24,128]{2,1,0:T(8,128)} copy(f32[48,24,128]{2,1,0:T(8,128)} %bitcast.9) | data formatting | bytes 1179648
  189.1 0.0 copy-done
  189.1 0.7 copy.16
Async XLA Ops:
  185.4 3.7 %copy-start = (f32[6,128,128]{2,1,0:T(8,128)S(1)}, f32[6,128,128]{2,1,0:T(8,128)}, u32[]{:S(2)}) copy-start(f32[6,128,128]{2,1,0:T(8,128)} %get-tuple-element.14) | copy-start | bytes 1179652

commit v3 on v2

--- a/solution.py
+++ b/solution.py
@@ -16,9 +16,28 @@
 WIDE = 1024
 TILE_ROWS = 384
 MESH = pl.DeviceIdType.MESH
-RIGHT, LEFT, TRI0, TRI1, GRAD0, GRAD1, BACK_L, BACK_R = range(8)
-PHASES = ((9, 80), (9, 80), (3, 32), (6, 48), (3, 32), (6, 48), (9, 80), (9, 80))
-PARTS = ((0, 1), (1, 2))
+RIGHT, LEFT, TRI, GRAD, BACK_L, BACK_R = range(6)
+A0, A1, A2, T0, T1, G0, G1, B0, B1, B2 = range(10)
+
+
+def some(array, first, last):
+    return tuple((array, block) for block in range(first, last))
+
+
+PHASES = (
+    some(RIGHT, 0, 4),
+    some(RIGHT, 4, 9) + some(LEFT, 8, 9),
+    some(LEFT, 0, 8),
+    some(TRI, 0, 6),
+    some(TRI, 6, 9),
+    some(GRAD, 0, 6),
+    some(GRAD, 6, 9),
+    some(BACK_L, 0, 8),
+    some(BACK_L, 8, 9) + some(BACK_R, 0, 5),
+    some(BACK_R, 5, 9),
+)
+WHERE = {item: (phase, k) for phase, items in enumerate(PHASES) for k, item in enumerate(items)}
+HELD = tuple((len(items) * 8 + 15) // 16 * 16 for items in PHASES)
 
 
 def nt(a, b):
@@ -27,6 +46,10 @@
 
 def nn(a, b):
     return lax.dot_general(a, b, (((1,), (0,)), ((), ())), preferred_element_type=F32)
+
+
+def tn(a, b):
+    return lax.dot_general(a, b, (((0,), (0,)), ((), ())), preferred_element_type=F32)
 
 
 def normalize(values):
@@ -86,10 +109,12 @@
     xb,
     inv,
     stack,
-    flat,
+    act,
+    picked,
     turned,
     left,
     right,
+    permuted,
     gmat,
     tri,
     gs,
@@ -99,10 +124,10 @@
     *rest,
 ):
     rest = list(rest)
-    ys, yr, zs, zr = ([rest.pop(0) for _ in PHASES] for _ in range(4))
-    sums = [[rest.pop(0) for _ in range(9)] for _ in range(2)]
+    ys, yr, zs, zr, flats = ([rest.pop(0) for _ in PHASES] for _ in range(5))
+    sums = [[rest.pop(0) for _ in range(8)] for _ in range(3)]
     y_send, y_recv, z_send, z_recv, s_send, s_recv = (rest.pop(0) for _ in range(6))
-    w_sems = [[rest.pop(0) for _ in range(10)] for _ in range(2)]
+    w_sems = [[rest.pop(0) for _ in range(8)] for _ in range(3)]
     local = rest.pop(0)
 
     r = lax.axis_index("row")
@@ -184,7 +209,8 @@
         zr[phase][z] = make(z)
 
     def z_wait(phase):
-        rows = PHASES[phase][1]
+        rows = HELD[phase]
+        flat = flats[phase]
 
         def receive(step):
             frm = next_z(Z - 2 - step)
@@ -194,61 +220,64 @@
         flat[at(z * (rows // 16), rows, 16), :] = zr[phase][z].astype(F32)
         loop(Z - 1, receive)
 
+    def y_fill(phase):
+        for k, (array, block) in enumerate(PHASES[phase]):
+            for other in range(G):
+                ys[phase][other, k] = act[array, block, other * 16 : other * 16 + 16]
+
     def z_start_up(phase):
-        blocks, rows = PHASES[phase]
+        blocks, rows = len(PHASES[phase]), HELD[phase]
 
         def spread(step):
-            flat[at(step, 16, 16), :] = yr[phase][step // blocks, step % blocks].astype(F32)
+            picked[at(step, 16, 16), :] = yr[phase][step // blocks, step % blocks].astype(F32)
 
         loop(G * blocks, spread)
-        z_start(phase, lambda to: flat[pl.ds(to, rows, stride=Z), :].astype(BF16))
+        z_start(phase, lambda to: picked[pl.ds(to, rows, stride=Z), :].astype(BF16))
 
     def z_start_back(phase):
-        rows = PHASES[phase][1]
-        z_start(phase, lambda to: flat[at(to * (rows // 16), rows, 16), :].astype(BF16))
+        rows = HELD[phase]
+        z_start(phase, lambda to: flats[phase][at(to * (rows // 16), rows, 16), :].astype(BF16))
 
     def y_start_back(phase):
-        blocks, rows = PHASES[phase]
+        blocks, rows = len(PHASES[phase]), HELD[phase]
 
         def body(step):
-            ys[phase][step // blocks, step % blocks] = flat[pl.ds(step, Z, stride=rows), :].astype(BF16)
+            values = flats[phase][pl.ds(step, Z, stride=rows), :]
+            ys[phase][step // blocks, step % blocks] = values.astype(BF16)
 
         loop(G * blocks, body)
         y_start(phase)
 
-    def split(part):
-        first, count = part
-        return lambda step: (step // count, first + step % count, step % count)
-
-    def turn_up(phase, part):
-        blocks, rows = PHASES[phase]
-
-        def body(step):
-            yy, row, own = split(part)(step)
-            pieces = [
-                flat[pl.ds((yy * 2 + hh) * blocks + own * 3 + b, Z, stride=rows), :]
-                for b in range(3)
-                for hh in range(2)
-            ]
-            pieces.append(jnp.zeros((32, C), F32))
-            turned[at(yy * 3 + row, C, C), :] = jnp.concatenate(pieces, axis=0).T
-
-        loop(Y * part[1], body)
-
-    def turn_back(phase, part):
-        blocks, rows = PHASES[phase]
-
-        def body(step):
-            yy, row, own = split(part)(step)
-            values = turned[at(yy * 3 + row, C, C), :].T
-            for b in range(3):
-                for hh in range(2):
-                    first = b * 32 + hh * 16
-                    flat[pl.ds((yy * 2 + hh) * blocks + own * 3 + b, Z, stride=rows), :] = values[
-                        first : first + 16
-                    ]
-
-        loop(Y * part[1], body)
+    def place(array, block, part):
+        phase, k = WHERE[array, block]
+        return flats[phase], pl.ds(part * len(PHASES[phase]) + k, Z, stride=HELD[phase])
+
+    def turn_up(array, rows):
+        for row in rows:
+
+            def body(yy, row=row):
+                pieces = []
+                for b in range(3):
+                    for hh in range(2):
+                        flat, held = place(array, row * 3 + b, yy * 2 + hh)
+                        pieces.append(flat[held, :])
+                pieces.append(jnp.zeros((32, C), F32))
+                turned[at(yy * 3 + row, C, C), :] = jnp.concatenate(pieces, axis=0).T
+
+            loop(Y, body)
+
+    def turn_back(array, rows):
+        for row in rows:
+
+            def body(yy, row=row):
+                values = turned[at(yy * 3 + row, C, C), :].T
+                for b in range(3):
+                    for hh in range(2):
+                        first = b * 32 + hh * 16
+                        flat, held = place(array, row * 3 + b, yy * 2 + hh)
+                        flat[held, :] = values[first : first + 16]
+
+            loop(Y, body)
 
     def low_columns(low):
         return at(low, C, C)
@@ -296,8 +325,8 @@
         s_wait(phase, ref, mate(1))
         passing_on(phase, ref).start()
 
-    def summing(which, rows):
-        a_s, a_r, b_s, b_r, c_s, c_r, d_s, d_r, e_r = sums[which]
+    def summing(which, first):
+        a_s, a_r, b_s, b_r, c_s, c_r, d_s, d_r = sums[which]
         sems = w_sems[which]
 
         def copy(step, src, dst, to, slot, device):
@@ -311,14 +340,13 @@
             )
 
         copies = (
-            lambda to, slot: copy(0, a_s.at[to], a_r.at[slot], to, slot, group(to)),
-            lambda to, slot: copy(1, b_s.at[to], b_r.at[slot], to, slot, shared(to)),
-            lambda to, slot: copy(2, c_s, c_r.at[slot], to, slot, along(to)),
-            lambda to, slot: copy(3, d_s, d_r.at[slot], to, slot, shared(to)),
-            lambda to, slot: copy(4, d_r, e_r.at[slot], to, slot, group(to)),
+            lambda to, slot: copy(0, a_s.at[to], a_r.at[slot], to, slot, along(to)),
+            lambda to, slot: copy(1, b_s, b_r.at[slot], to, slot, group(to)),
+            lambda to, slot: copy(2, c_s, c_r.at[slot], to, slot, shared(to)),
+            lambda to, slot: copy(3, d_s, d_r.at[slot], to, slot, along(to)),
         )
-        others = ((G - 1, next_g), (S - 1, mate), (Z - 1, next_z), (S - 1, mate), (G - 1, next_g))
-        mine = (g, s, z, s, g)
+        others = ((Z - 1, next_z), (G - 1, next_g), (S - 1, mate), (Z - 1, next_z))
+        mine = (z, g, s, z)
 
         def start(step):
             count, other = others[step]
@@ -328,45 +356,41 @@
             count, other = others[step]
             loop(count, lambda d: copies[step](other(d), other(d)).wait_recv())
 
-        def first():
+        def one():
+            for k in range(Z):
+                rows, columns = (k % 8) * 16, (first + k // 8) * C
+                a_s[k] = gwin[rows : rows + 16, columns : columns + C].astype(BF16)
             start(0)
-            a_r[g] = a_s[g]
-
-        def second():
+            a_r[z] = a_s[z]
+
+        def two():
             wait(0)
-            total = sum(a_r[k].astype(F32) for k in range(G))
-            for k in range(S):
-                b_s[k] = total[k * (rows // S) : (k + 1) * (rows // S)]
+            b_s[...] = sum(a_r[k].astype(F32) for k in range(Z))
             start(1)
-            b_r[s] = b_s[s]
-
-        def third():
+            b_r[g] = b_s[...]
+
+        def three():
             wait(1)
-            c_s[...] = sum(b_r[k] for k in range(S))
+            c_s[...] = sum(b_r[k] for k in range(G))
             start(2)
-            c_r[z] = c_s[...]
-
-        def fourth():
+            c_r[s] = c_s[...]
+
+        def four():
             wait(2)
-            d_s[...] = sum(c_r[k] for k in range(Z)) * (1.0 / 768.0)
+            d_s[...] = (sum(c_r[k] for k in range(S)) * (1.0 / 768.0)).astype(BF16)
             start(3)
-            d_r[s] = d_s[...]
-
-        def fifth():
+            d_r[z] = d_s[...]
+
+        def five():
             wait(3)
-            start(4)
-            e_r[g] = d_r[...]
-
-        def last(write):
-            wait(4)
-            for k in range(G):
-                write(k, e_r[k].reshape(rows, C))
+            for k in range(Z):
+                gw_ref[first + k // 8, (k % 8) * 16 : (k % 8) * 16 + 16] = d_r[k].astype(F32)
 
         def sent():
             for step, (count, other) in enumerate(others):
                 loop(count, lambda d, c=copies[step], o=other: c(o(d), o(d)).wait_send())
 
-        return first, second, third, fourth, fifth, last, sent
+        return one, two, three, four, five, sent
 
     for m in range(6):
         wt[m * C : (m + 1) * C] = weights_ref[m].astype(F32).T.astype(BF16)
@@ -385,35 +409,44 @@
 
     load_pair.wait()
 
-    def project(row):
+    def activate(block, array):
+        first = 2 * array * C
+        p = nn(wt[first : first + 2 * C], xb[block])
+        proj[block, first : first + 2 * C] = p
+        value = mask_ref[block] * jax.nn.sigmoid(p[C:]) * p[:C]
+        act[RIGHT if array else LEFT, block] = value.astype(BF16)
+
+    def project_right(row):
         values = tile_rows(pair_v, row)
         for b in range(3):
             block = row * 3 + b
             normed, inverse = normalize(block_of(values, b))
-            rounded = normed.astype(BF16)
             xn[block] = normed
-            xb[block] = rounded
+            xb[block] = normed.astype(BF16)
             inv[block] = inverse
-            p = nn(wt[: 5 * C], rounded)
-            proj[block] = p
-            mask = mask_ref[block]
-            left_act = (mask * jax.nn.sigmoid(p[C : 2 * C]) * p[:C]).astype(BF16)
-            right_act = (mask * jax.nn.sigmoid(p[3 * C : 4 * C]) * p[2 * C : 3 * C]).astype(BF16)
-            for k in range(G):
-                ys[LEFT][k, block] = left_act[k * 16 : k * 16 + 16]
-                ys[RIGHT][k, block] = right_act[k * 16 : k * 16 + 16]
-
-    loop(3, project)
+            activate(block, 1)
+
+    def project_gate(block):
+        proj[block, 4 * C :] = jax.nn.sigmoid(nn(wt[4 * C : 5 * C], xb[block]))
+
+    loop(3, project_right)
+    y_fill(A0)
     pl.semaphore_wait(barrier, Z + G + S - 3)
 
-    whole = (0, 3)
-    y_start(RIGHT)
-    y_wait(RIGHT)
-    y_start(LEFT)
-    flat[G * BLOCKS * Z :, :] = jnp.zeros((8 * Z, C), F32)
-    z_start_up(RIGHT)
-    y_wait(LEFT)
-    z_start_up(LEFT)
+    whole = range(3)
+    y_start(A0)
+    loop(BLOCKS, lambda block: activate(block, 0))
+    y_fill(A1)
+    y_start(A1)
+    y_wait(A0)
+    z_start_up(A0)
+    y_fill(A2)
+    y_wait(A1)
+    y_start(A2)
+    z_start_up(A1)
+    y_wait(A2)
+    z_start_up(A2)
+    loop(BLOCKS, project_gate)
 
     def write_to(ref, *index):
         def write(columns, value):
@@ -421,14 +454,16 @@
 
         return write
 
-    z_wait(RIGHT)
-    turn_up(RIGHT, whole)
+    z_wait(A0)
+    turn_up(RIGHT, range(1))
+    z_wait(A1)
+    turn_up(RIGHT, range(1, 3))
     matrix(write_to(right, s))
     share(0, right)
     load_cot.wait()
     load_order.wait()
     pass_on(0, right)
-    z_wait(LEFT)
+    z_wait(A2)
     turn_up(LEFT, whole)
     matrix(write_to(left, s))
 
@@ -444,14 +479,21 @@
     from_matrix(
         lambda columns: sum(nn(tri[k, :, :ROWS], order[k, :, columns]) for k in range(S))
     )
-    for part, phase in enumerate((TRI0, TRI1)):
-        turn_back(phase, PARTS[part])
-        z_start_back(phase)
+    turn_back(TRI, range(2))
+    z_start_back(T0)
+    turn_back(TRI, range(2, 3))
+    z_start_back(T1)
     share(1, left)
 
-    def tile(phase, back, part):
+    def permute(low):
+        rows = low_columns(low)
+        permuted[rows, :] = sum(tn(order[k, :, rows], right[k]) for k in range(S)).astype(BF16)
+
+    loop(8, permute)
+
+    def tile(phase, first, count):
         def body(step):
-            row = part[0] + step
+            row = first + step
             cotangent = tile_rows(cot_v, row)
             updates = []
             for b in range(3):
@@ -460,7 +502,7 @@
                 normed, inverse = normalize(values.astype(F32))
                 rounded = normed.astype(BF16)
                 linear = nn(wt[5 * C :], rounded)
-                gate = jax.nn.sigmoid(proj[block, 4 * C :])
+                gate = proj[block, 4 * C :]
                 updates.append(gate * linear)
                 upstream = block_of(cotangent, b)
                 grad_linear = (upstream * gate).astype(BF16)
@@ -471,39 +513,39 @@
                 grad_xout = nn(weights_ref[5], grad_linear)
                 grad = norm_backward(grad_xout, normed, inverse).astype(BF16)
                 for k in range(G):
-                    ys[back][k, own] = grad[k * 16 : k * 16 + 16]
+                    ys[phase + G0 - T0][k, own] = grad[k * 16 : k * 16 + 16]
             upd_v[at(row, TILE_ROWS, TILE_ROWS), :] = rows_of(updates).astype(BF16)
 
-        loop(part[1], body)
-
-    z_wait(TRI0)
-    y_start_back(TRI0)
-    y_wait(TRI0)
-    tile(TRI0, GRAD0, PARTS[0])
-    y_start(GRAD0)
-    z_wait(TRI1)
-    y_start_back(TRI1)
-    y_wait(GRAD0)
-    z_start_up(GRAD0)
-    y_wait(TRI1)
-    tile(TRI1, GRAD1, PARTS[1])
-    y_start(GRAD1)
+        loop(count, body)
+
+    z_wait(T0)
+    y_start_back(T0)
+    y_wait(T0)
+    tile(T0, 0, 2)
+    y_start(G0)
+    z_wait(T1)
+    y_start_back(T1)
+    y_wait(G0)
+    z_start_up(G0)
+    y_wait(T1)
+    tile(T1, 2, 1)
+    y_start(G1)
     store_upd = pltpu.make_async_copy(upd_v, upd_hbm, local.at[0])
     store_upd.start()
-    early = summing(0, 32)
-    for k in range(G):
-        m, first = 4 + k // 4, (k % 4) * 32
-        sums[0][0][k] = gwin[first : first + 32, m * C : (m + 1) * C].astype(BF16)
-    y_wait(GRAD1)
-    z_start_up(GRAD1)
+    early = summing(0, 4)
+    y_wait(G1)
+    z_start_up(G1)
     early[0]()
     pass_on(1, left)
-    z_wait(GRAD0)
-    turn_up(GRAD0, PARTS[0])
-    early[1]()
-    z_wait(GRAD1)
-    turn_up(GRAD1, PARTS[1])
+    z_wait(G0)
+    turn_up(GRAD, range(2))
+    z_wait(G1)
+    turn_up(GRAD, range(2, 3))
     matrix(write_to(gmat))
+
+    from_matrix(lambda columns: nn(gmat[...], permuted[:, columns]))
+    turn_back(BACK_L, whole)
+    z_start_back(B0)
 
     def columns_of(part):
         gts[part, :, :ROWS] = nt(order[part], gmat[...]).astype(BF16)
@@ -515,17 +557,7 @@
 
     loop(S - 1, lambda d: give(d).start())
     gtr[s] = gts[s]
-
-    def rows_for(part):
-        gs[part, :, :ROWS] = nt(gmat[...], order[part]).astype(BF16)
-
-    loop(S, rows_for)
-    from_matrix(
-        lambda columns: sum(nn(gs[k, :, :ROWS], right[k, :, columns]) for k in range(S))
-    )
-    turn_back(BACK_L, whole)
-    z_start_back(BACK_L)
-    early[2]()
+    early[1]()
     s_wait(1, left, mate(0))
     s_wait(1, left, mate(2))
     loop(S - 1, lambda d: s_wait(2, gtr, mate(d)))
@@ -533,44 +565,48 @@
         lambda columns: sum(nn(gtr[k, :, :ROWS], left[k, :, columns]) for k in range(S))
     )
     turn_back(BACK_R, whole)
-    z_start_back(BACK_R)
-    early[3]()
-
-    def grads_of(phase, array):
-        def body(block):
-            values = jnp.concatenate([yr[phase][k, block] for k in range(G)], axis=0)
+    z_start_back(B1)
+    z_start_back(B2)
+    early[2]()
+
+    def grads_of(array, phase, first, block_first, count):
+        def body(step):
+            block, own = block_first + step, first + step
+            values = jnp.concatenate([yr[phase][k, own] for k in range(G)], axis=0)
             upstream = values.astype(F32) * mask_ref[block]
-            first = 2 * array * C
-            value = proj[block, first : first + C]
-            gate = jax.nn.sigmoid(proj[block, first + C : first + 2 * C])
+            row = 2 * array * C
+            value = proj[block, row : row + C]
+            gate = jax.nn.sigmoid(proj[block, row + C : row + 2 * C])
             pieces = (upstream * gate, upstream * value * gate * (1.0 - gate))
             for k in range(2):
                 piece = pieces[k].astype(BF16)
-                columns = slice(first + k * C, first + (k + 1) * C)
+                columns = slice(row + k * C, row + (k + 1) * C)
                 stack[block, columns] = piece
                 gwin[:, columns] += nt(xb[block], piece)
 
-        loop(BLOCKS, body)
-
-    z_wait(BACK_L)
-    y_start_back(BACK_L)
+        loop(count, body)
+
+    z_wait(B0)
+    y_start_back(B0)
+    early[3]()
+    y_wait(B0)
+    grads_of(0, B0, 0, 0, 8)
+    z_wait(B1)
+    y_start_back(B1)
+    y_wait(B1)
+    grads_of(0, B1, 0, 8, 1)
+    middle = summing(1, 0)
+    middle[0]()
+    grads_of(1, B1, 1, 0, 5)
+    z_wait(B2)
+    y_start_back(B2)
     early[4]()
-    y_wait(BACK_L)
-    grads_of(BACK_L, 0)
-
-    def write_early(k, rows):
-        gw_ref[4 + k // 4, (k % 4) * 32 : (k % 4) * 32 + 32] = rows
-
-    early[5](write_early)
-    z_wait(BACK_R)
-    y_start_back(BACK_R)
-    y_wait(BACK_R)
-    grads_of(BACK_R, 1)
-    late = summing(1, 64)
-    for k in range(G):
-        m, first = k // 2, (k % 2) * 64
-        sums[1][0][k] = gwin[first : first + 64, m * C : (m + 1) * C].astype(BF16)
+    middle[1]()
+    y_wait(B2)
+    grads_of(1, B2, 0, 5, 4)
+    late = summing(2, 2)
     late[0]()
+    middle[2]()
 
     def store_gpair(row):
         rows = at(row, TILE_ROWS, TILE_ROWS)
@@ -585,13 +621,12 @@
         store_gpair(row).start()
 
     loop(3, finish)
-    for step in range(1, 5):
-        late[step]()
-
-    def write_late(k, rows):
-        gw_ref[k // 2, (k % 2) * 64 : (k % 2) * 64 + 64] = rows
-
-    late[5](write_late)
+    late[1]()
+    middle[3]()
+    late[2]()
+    late[3]()
+    middle[4]()
+    late[4]()
 
     store_upd.wait()
     loop(3, lambda row: store_gpair(row).wait())
@@ -603,8 +638,9 @@
             s_copy(phase, ref.at[s], ref.at[s], s, mate(d)).wait_send()
         passing_on(phase, ref).wait_send()
     loop(S - 1, lambda d: give(d).wait_send())
-    early[6]()
-    late[6]()
+    early[5]()
+    middle[5]()
+    late[5]()
 
 
 def on_device(pair, pair_mask, weights, cotangent):
@@ -616,20 +652,14 @@
     def sems(*shape):
         return [pltpu.SemaphoreType.DMA(shape)] * 2
 
-    def sum_buffers(rows):
-        small = rows // S
-        return [
-            *[pltpu.VMEM((G, rows, C), BF16)] * 2,
-            *[pltpu.VMEM((S, small, C), F32)] * 2,
-            pltpu.VMEM((small, C), F32),
-            pltpu.VMEM((Z, small, C), F32),
-            pltpu.VMEM((small, C), F32),
-            pltpu.VMEM((S, small, C), F32),
-            pltpu.VMEM((G, S, small, C), F32),
-        ]
-
-    y_buffers = [pltpu.VMEM((G, blocks, 16, C), BF16) for blocks, _ in PHASES]
-    z_buffers = [pltpu.VMEM((Z, rows, C), BF16) for _, rows in PHASES]
+    def sum_buffers():
+        one = [pltpu.VMEM((16, C), F32), pltpu.VMEM((G, 16, C), F32)]
+        two = [pltpu.VMEM((16, C), F32), pltpu.VMEM((S, 16, C), F32)]
+        last = [pltpu.VMEM((16, C), BF16), pltpu.VMEM((Z, 16, C), BF16)]
+        return [pltpu.VMEM((Z, 16, C), BF16)] * 2 + one + two + last
+
+    y_buffers = [pltpu.VMEM((G, len(items), 16, C), BF16) for items in PHASES]
+    z_buffers = [pltpu.VMEM((Z, rows, C), BF16) for rows in HELD]
     update, grad_pair, grad_weights = pl.pallas_call(
         kernel,
         out_shape=(
@@ -652,10 +682,12 @@
             pltpu.VMEM((BLOCKS, C, C), BF16),
             pltpu.VMEM((BLOCKS, 1, C), F32),
             pltpu.VMEM((BLOCKS, 5 * C, C), BF16),
-            pltpu.VMEM((Z * 80, C), F32),
+            pltpu.VMEM((2, BLOCKS, C, C), BF16),
+            pltpu.VMEM((Z * max(HELD), C), F32),
             pltpu.VMEM((12 * C, C), F32),
             pltpu.VMEM((S, ROWS, WIDE), BF16),
             pltpu.VMEM((S, ROWS, WIDE), BF16),
+            pltpu.VMEM((WIDE, WIDE), BF16),
             pltpu.VMEM((ROWS, WIDE), BF16),
             *[pltpu.VMEM((S, ROWS, 256), BF16)] * 4,
             pltpu.VMEM((C, 6 * C), F32),
@@ -663,12 +695,12 @@
             *y_buffers,
             *z_buffers,
             *z_buffers,
-            *sum_buffers(32),
-            *sum_buffers(64),
+            *[pltpu.VMEM((Z * rows, C), F32) for rows in HELD],
+            *[buffer for _ in range(3) for buffer in sum_buffers()],
             *sems(len(PHASES), G),
             *sems(len(PHASES), Z),
             *sems(3, S),
-            *[sem for _ in range(2) for n in (G, S, Z, S, G) for sem in sems(n)],
+            *[sem for _ in range(3) for n in (Z, G, S, Z) for sem in sems(n)],
             pltpu.SemaphoreType.DMA((6,)),
         ],
         compiler_params=pltpu.CompilerParams(

time: 190 us -> 181 us (0.953)
  Pallas kernels: 183 us -> 174 us
    pallas_call x1, Pallas kernels: 183 us -> 174 us  [on_device(): pl.pallas_call(kernel, out_shape=(jax.ShapeDtypeStruct((pixels, C), BF16)...]
where the time goes in v3:
time: 181 us
  Pallas kernels  174 us (96%)
  local copies, waits for them, and re-layouts  5.3 us (3%)
    pallas_call x1, Pallas kernels, on_device(): pl.pallas_call(kernel, out_shape=(jax.ShapeDtypeStruct((pixels, C), BF16)...  174 us
    unnamed x5, local copies, waits for them, and re-layouts  4.42 us

profile of v3, /device:TPU:1, one launch (start us, length us, event | category | flops | bytes accessed | tf_op | source)
XLA Modules:
  0.0 180.8 jit_solution(18027082568685653)
XLA Ops:
  0.6 0.7 convert_element_type.3
  1.3 0.1 reshape.26
  1.4 0.1 copy.9
  1.5 0.7 reshape.30.mask_ref
  2.2 174.1 %shard_map.76 = (bf16[1152,128]{1,0:T(8,128)(2,1)}, f32[1152,128]{1,0:T(8,128)}, f32[6,128,128]{2,1,0:T(8,128)}) custom-call(bf16[1152,128]{1,0:T(8,128)(2,1)} %bitcast.11, bf16[1152,128]{1,0:T(8,128)(2,1)} %bitcast.12, bf16[4,192,1024]{2,1,0:T(8,128)(2,1)} %constant.2.clone.order_hbm, f32[9,1,128]{2,1,0:T(1,128)} %reshape.30.mask_ref, ...), custom_call_target="tpu_custom_call" | custom-call | tf_op jit(solution)/shard_map/pallas_call | solution.py:663
  176.4 0.0 copy-start
  176.4 1.8 copy.14
  178.1 1.9 %copy.15 = f32[48,24,128]{2,1,0:T(8,128)} copy(f32[48,24,128]{2,1,0:T(8,128)} %bitcast.9) | data formatting | bytes 1179648
  180.0 0.0 copy-done
  180.1 0.7 copy.16
Async XLA Ops:
  176.4 3.7 %copy-start = (f32[6,128,128]{2,1,0:T(8,128)S(1)}, f32[6,128,128]{2,1,0:T(8,128)}, u32[]{:S(2)}) copy-start(f32[6,128,128]{2,1,0:T(8,128)} %get-tuple-element.14) | copy-start | bytes 1179652

commit v4 on v3

--- a/solution.py
+++ b/solution.py
@@ -17,7 +17,7 @@
 TILE_ROWS = 384
 MESH = pl.DeviceIdType.MESH
 RIGHT, LEFT, TRI, GRAD, BACK_L, BACK_R = range(6)
-A0, A1, A2, T0, T1, G0, G1, B0, B1, B2 = range(10)
+A0, A1, A2, A3, T0, T1, T2, G0, G1, G2, B0, B1, B2, B3 = range(14)
 
 
 def some(array, first, last):
@@ -25,14 +25,18 @@
 
 
 PHASES = (
-    some(RIGHT, 0, 4),
-    some(RIGHT, 4, 9) + some(LEFT, 8, 9),
-    some(LEFT, 0, 8),
-    some(TRI, 0, 6),
+    some(RIGHT, 0, 6),
+    some(RIGHT, 6, 9) + some(LEFT, 0, 1),
+    some(LEFT, 1, 3),
+    some(LEFT, 3, 9),
+    some(TRI, 0, 2),
+    some(TRI, 2, 6),
     some(TRI, 6, 9),
-    some(GRAD, 0, 6),
+    some(GRAD, 0, 2),
+    some(GRAD, 2, 6),
     some(GRAD, 6, 9),
-    some(BACK_L, 0, 8),
+    some(BACK_L, 0, 6),
+    some(BACK_L, 6, 8),
     some(BACK_L, 8, 9) + some(BACK_R, 0, 5),
     some(BACK_R, 5, 9),
 )
@@ -46,10 +50,6 @@
 
 def nn(a, b):
     return lax.dot_general(a, b, (((1,), (0,)), ((), ())), preferred_element_type=F32)
-
-
-def tn(a, b):
-    return lax.dot_general(a, b, (((0,), (0,)), ((), ())), preferred_element_type=F32)
 
 
 def normalize(values):
@@ -72,7 +72,7 @@
     place = (low * 128 + block * 32 + tile).reshape(-1)
     y, s, inner = residue // 192, residue // 48 % 4, residue % 48
     order = np.zeros((S, ROWS, WIDE), np.float32)
-    order[s, y * 48 + inner, place] = 1
+    order[s, inner // 16 * 64 + y * 16 + inner % 16, place] = 1
     return order.astype(jnp.bfloat16)
 
 
@@ -116,11 +116,15 @@
     right,
     permuted,
     gmat,
-    tri,
+    residues,
     gs,
-    gts,
-    gtr,
+    gts0,
+    gtr0,
+    gts1,
+    gtr1,
     gwin,
+    upstream,
+    updates,
     *rest,
 ):
     rest = list(rest)
@@ -215,10 +219,14 @@
         def receive(step):
             frm = next_z(Z - 2 - step)
             z_copy(phase, frm, frm).wait_recv()
-            flat[at(frm * (rows // 16), rows, 16), :] = zr[phase][frm].astype(F32)
-
-        flat[at(z * (rows // 16), rows, 16), :] = zr[phase][z].astype(F32)
+
+        def widen(step):
+            for k in range(4):
+                frm = step * 4 + k
+                flat[at(frm * (rows // 16), rows, 16), :] = zr[phase][frm].astype(F32)
+
         loop(Z - 1, receive)
+        loop(Z // 4, widen)
 
     def y_fill(phase):
         for k, (array, block) in enumerate(PHASES[phase]):
@@ -228,10 +236,11 @@
     def z_start_up(phase):
         blocks, rows = len(PHASES[phase]), HELD[phase]
 
-        def spread(step):
-            picked[at(step, 16, 16), :] = yr[phase][step // blocks, step % blocks].astype(F32)
-
-        loop(G * blocks, spread)
+        def spread(k):
+            for other in range(G):
+                picked[at(other * blocks + k, 16, 16), :] = yr[phase][other, k].astype(F32)
+
+        loop(blocks, spread)
         z_start(phase, lambda to: picked[pl.ds(to, rows, stride=Z), :].astype(BF16))
 
     def z_start_back(phase):
@@ -241,11 +250,12 @@
     def y_start_back(phase):
         blocks, rows = len(PHASES[phase]), HELD[phase]
 
-        def body(step):
-            values = flats[phase][pl.ds(step, Z, stride=rows), :]
-            ys[phase][step // blocks, step % blocks] = values.astype(BF16)
-
-        loop(G * blocks, body)
+        def body(k):
+            for other in range(G):
+                values = flats[phase][pl.ds(other * blocks + k, Z, stride=rows), :]
+                ys[phase][other, k] = values.astype(BF16)
+
+        loop(blocks, body)
         y_start(phase)
 
     def place(array, block, part):
@@ -255,44 +265,53 @@
     def turn_up(array, rows):
         for row in rows:
 
-            def body(yy, row=row):
+            for yy in range(Y):
                 pieces = []
                 for b in range(3):
                     for hh in range(2):
-                        flat, held = place(array, row * 3 + b, yy * 2 + hh)
-                        pieces.append(flat[held, :])
+                        flat, spot = place(array, row * 3 + b, yy * 2 + hh)
+                        pieces.append(flat[spot, :])
                 pieces.append(jnp.zeros((32, C), F32))
-                turned[at(yy * 3 + row, C, C), :] = jnp.concatenate(pieces, axis=0).T
-
-            loop(Y, body)
+                turned[(row * Y + yy) * C : (row * Y + yy + 1) * C, :] = jnp.concatenate(pieces, axis=0).T
 
     def turn_back(array, rows):
         for row in rows:
 
-            def body(yy, row=row):
-                values = turned[at(yy * 3 + row, C, C), :].T
+            for yy in range(Y):
+                values = turned[(row * Y + yy) * C : (row * Y + yy + 1) * C, :].T
                 for b in range(3):
                     for hh in range(2):
                         first = b * 32 + hh * 16
-                        flat, held = place(array, row * 3 + b, yy * 2 + hh)
-                        flat[held, :] = values[first : first + 16]
-
-            loop(Y, body)
+                        flat, spot = place(array, row * 3 + b, yy * 2 + hh)
+                        flat[spot, :] = values[first : first + 16]
 
     def low_columns(low):
         return at(low, C, C)
 
-    def matrix(write):
-        def body(low):
-            write(low_columns(low), turned[pl.ds(low, ROWS, stride=8), :].astype(BF16))
-
-        loop(8, body)
-
-    def from_matrix(make):
-        def body(low):
-            turned[pl.ds(low, ROWS, stride=8), :] = make(low_columns(low))
-
-        loop(8, body)
+    def held(rows):
+        size = 64 * len(rows)
+        return slice(rows[0] * 64, rows[0] * 64 + size), lambda low: pl.ds(
+            rows[0] * 512 + low, size, stride=8
+        )
+
+    def matrix(ref, rows):
+        kept, where = held(rows)
+
+        def body(pair):
+            for low in (2 * pair, 2 * pair + 1):
+                ref[kept, low_columns(low)] = turned[where(low), :].astype(BF16)
+
+        loop(4, body)
+
+    def from_matrix(rows, make):
+        kept, where = held(rows)
+
+        def body(pair):
+            values = make(kept, at(pair, 2 * C, 2 * C))
+            turned[where(2 * pair), :] = values[:, :C]
+            turned[where(2 * pair + 1), :] = values[:, C:]
+
+        loop(4, body)
 
     def s_copy(phase, src, dst, slot, to):
         return pltpu.make_async_remote_copy(
@@ -304,26 +323,28 @@
             device_id_type=MESH,
         )
 
-    def share(phase, ref):
-        s_copy(phase, ref.at[s], ref.at[s], s, mate(1)).start()
-        s_copy(phase, ref.at[s], ref.at[s], s, mate(0)).start()
-
-    def passing_on(phase, ref):
+    def share(phase, ref, rows):
+        part = ref.at[s, rows]
+        s_copy(phase, part, part, s, mate(1)).start()
+        s_copy(phase, part, part, s, mate(0)).start()
+
+    def passing_on(phase, ref, rows):
         return pltpu.make_async_remote_copy(
-            src_ref=ref.at[mate(1)],
-            dst_ref=ref.at[mate(1)],
+            src_ref=ref.at[mate(1), rows],
+            dst_ref=ref.at[mate(1), rows],
             send_sem=s_send.at[phase, mate(2)],
             recv_sem=s_recv.at[phase, mate(1)],
             device_id=shared(mate(0)),
             device_id_type=MESH,
         )
 
-    def s_wait(phase, ref, slot):
-        s_copy(phase, ref.at[slot], ref.at[slot], slot, slot).wait_recv()
-
-    def pass_on(phase, ref):
-        s_wait(phase, ref, mate(1))
-        passing_on(phase, ref).start()
+    def s_wait(phase, ref, slot, rows):
+        part = ref.at[slot, rows]
+        s_copy(phase, part, part, slot, slot).wait_recv()
+
+    def pass_on(phase, ref, rows):
+        s_wait(phase, ref, mate(1), rows)
+        passing_on(phase, ref, rows).start()
 
     def summing(which, first):
         a_s, a_r, b_s, b_r, c_s, c_r, d_s, d_r = sums[which]
@@ -433,151 +454,198 @@
     y_fill(A0)
     pl.semaphore_wait(barrier, Z + G + S - 3)
 
-    whole = range(3)
     y_start(A0)
     loop(BLOCKS, lambda block: activate(block, 0))
     y_fill(A1)
     y_start(A1)
+    y_fill(A2)
+    y_fill(A3)
     y_wait(A0)
     z_start_up(A0)
-    y_fill(A2)
+    y_start(A2)
     y_wait(A1)
-    y_start(A2)
     z_start_up(A1)
+    y_start(A3)
     y_wait(A2)
     z_start_up(A2)
+    y_wait(A3)
+    z_start_up(A3)
     loop(BLOCKS, project_gate)
-
-    def write_to(ref, *index):
-        def write(columns, value):
-            ref[(*index, slice(None), columns)] = value
-
-        return write
-
+    load_cot.wait()
+
+    def turn_cotangent(row):
+        values = tile_rows(cot_v, row)
+        for b in range(3):
+            upstream[row * 3 + b] = block_of(values, b)
+
+    loop(3, turn_cotangent)
+    load_order.wait()
+    whole, two, last = range(3), range(2), range(2, 3)
+    most, least, full = slice(0, 128), slice(128, 192), slice(0, 192)
     z_wait(A0)
-    turn_up(RIGHT, range(1))
+    turn_up(RIGHT, two)
+    matrix(right.at[s], two)
+    share(0, right, most)
     z_wait(A1)
-    turn_up(RIGHT, range(1, 3))
-    matrix(write_to(right, s))
-    share(0, right)
-    load_cot.wait()
-    load_order.wait()
-    pass_on(0, right)
+    turn_up(RIGHT, last)
+    matrix(right.at[s], last)
+    share(1, right, least)
+    pass_on(0, right, most)
     z_wait(A2)
-    turn_up(LEFT, whole)
-    matrix(write_to(left, s))
-
-    def triangle(part):
-        tri[part, :, :ROWS] = nt(left[s], right[part]).astype(BF16)
-
-    triangle(s)
-    triangle(mate(1))
-    s_wait(0, right, mate(0))
-    triangle(mate(0))
-    s_wait(0, right, mate(2))
-    triangle(mate(2))
-    from_matrix(
-        lambda columns: sum(nn(tri[k, :, :ROWS], order[k, :, columns]) for k in range(S))
-    )
-    turn_back(TRI, range(2))
+    turn_up(LEFT, range(1))
+    matrix(left.at[s], range(1))
+    pass_on(1, right, least)
+
+    def natural(part):
+        for row in range(3):
+            for yy in range(Y):
+                first = row * 64 + yy * 16
+                to = pl.ds(pl.multiple_of(part * 48 + yy * ROWS + row * 16, 16), 16)
+                for low in range(8):
+                    values = right[part, first : first + 16, low * C : low * C + C]
+                    residues[low, to, :] = values.astype(F32)
+
+    def permute(low):
+        for b in range(3):
+            rows = at(low * 4 + b, 32, 32)
+            for k in range(8):
+                values = residues[k, pl.ds(low + 8 * b, 32, stride=24), :]
+                permuted[rows, k * C : k * C + C] = values.astype(BF16)
+        permuted[at(low * 4 + 3, 32, 32), :] = jnp.zeros((32, WIDE), BF16)
+
+    def triangle(rows):
+        from_matrix(rows, lambda kept, columns: nt(left[s, kept], permuted[columns, :]))
+        turn_back(TRI, rows)
+
+    for d in (0, 2):
+        s_wait(0, right, mate(d), most)
+        s_wait(1, right, mate(d), least)
+    loop(S, natural)
+    loop(8, permute)
+    triangle(range(1))
     z_start_back(T0)
-    turn_back(TRI, range(2, 3))
+    z_wait(A3)
+    turn_up(LEFT, range(1, 3))
+    matrix(left.at[s], range(1, 3))
+    triangle(range(1, 2))
     z_start_back(T1)
-    share(1, left)
-
-    def permute(low):
-        rows = low_columns(low)
-        permuted[rows, :] = sum(tn(order[k, :, rows], right[k]) for k in range(S)).astype(BF16)
-
-    loop(8, permute)
-
-    def tile(phase, first, count):
-        def body(step):
-            row = first + step
-            cotangent = tile_rows(cot_v, row)
-            updates = []
-            for b in range(3):
-                block, own = row * 3 + b, step * 3 + b
-                values = jnp.concatenate([yr[phase][k, own] for k in range(G)], axis=0)
-                normed, inverse = normalize(values.astype(F32))
-                rounded = normed.astype(BF16)
-                linear = nn(wt[5 * C :], rounded)
-                gate = proj[block, 4 * C :]
-                updates.append(gate * linear)
-                upstream = block_of(cotangent, b)
-                grad_linear = (upstream * gate).astype(BF16)
-                logit = (upstream * linear * gate * (1.0 - gate)).astype(BF16)
-                stack[block, 4 * C :] = logit
-                gwin[:, 4 * C : 5 * C] += nt(xb[block], logit)
-                gwin[:, 5 * C :] += nt(rounded, grad_linear)
-                grad_xout = nn(weights_ref[5], grad_linear)
-                grad = norm_backward(grad_xout, normed, inverse).astype(BF16)
-                for k in range(G):
-                    ys[phase + G0 - T0][k, own] = grad[k * 16 : k * 16 + 16]
-            upd_v[at(row, TILE_ROWS, TILE_ROWS), :] = rows_of(updates).astype(BF16)
-
-        loop(count, body)
+    triangle(last)
+    z_start_back(T2)
+
+    def tile(phase, first):
+        def body(own):
+            block = first + own
+            values = jnp.concatenate([yr[phase][k, own] for k in range(G)], axis=0)
+            normed, inverse = normalize(values.astype(F32))
+            rounded = normed.astype(BF16)
+            linear = nn(wt[5 * C :], rounded)
+            gate = proj[block, 4 * C :]
+            updates[block] = gate * linear
+            grad_linear = (upstream[block] * gate).astype(BF16)
+            logit = (upstream[block] * linear * gate * (1.0 - gate)).astype(BF16)
+            stack[block, 4 * C :] = logit
+            gwin[:, 4 * C : 5 * C] += nt(xb[block], logit)
+            gwin[:, 5 * C :] += nt(rounded, grad_linear)
+            grad_xout = nn(weights_ref[5], grad_linear)
+            grad = norm_backward(grad_xout, normed, inverse).astype(BF16)
+            for k in range(G):
+                ys[phase + G0 - T0][k, own] = grad[k * 16 : k * 16 + 16]
+
+        loop(len(PHASES[phase]), body)
 
     z_wait(T0)
     y_start_back(T0)
+    share(2, left, full)
     y_wait(T0)
-    tile(T0, 0, 2)
+    tile(T0, 0)
     y_start(G0)
     z_wait(T1)
     y_start_back(T1)
     y_wait(G0)
     z_start_up(G0)
+    z_wait(T2)
+    y_start_back(T2)
     y_wait(T1)
-    tile(T1, 2, 1)
+    tile(T1, 2)
     y_start(G1)
+    y_wait(T2)
+    tile(T2, 6)
+    y_start(G2)
+    y_wait(G1)
+    z_start_up(G1)
+    y_wait(G2)
+    z_start_up(G2)
+    early = summing(0, 4)
+    early[0]()
+
+    def update_rows(row):
+        rows = rows_of([updates[row * 3 + b] for b in range(3)])
+        upd_v[at(row, TILE_ROWS, TILE_ROWS), :] = rows.astype(BF16)
+
+    loop(3, update_rows)
     store_upd = pltpu.make_async_copy(upd_v, upd_hbm, local.at[0])
     store_upd.start()
-    early = summing(0, 4)
-    y_wait(G1)
-    z_start_up(G1)
-    early[0]()
-    pass_on(1, left)
+    pass_on(2, left, full)
+
+    def left_gradient(rows):
+        turn_up(GRAD, rows)
+        matrix(gmat, rows)
+        from_matrix(rows, lambda kept, columns: nn(gmat[kept], permuted[:, columns]))
+        turn_back(BACK_L, rows)
+
+    def give(which, d):
+        src, dst = (gts0, gtr0) if which == 0 else (gts1, gtr1)
+        return s_copy(3 + which, src.at[mate(d)], dst.at[s], s, mate(d))
+
+    def columns_of(part):
+        gts0[part] = nt(order[part], gmat[:128]).astype(BF16)
+
+    def last_columns_of(part):
+        gts1[part, :, :64] = nt(order[part], gmat[128:]).astype(BF16)
+
     z_wait(G0)
-    turn_up(GRAD, range(2))
     z_wait(G1)
-    turn_up(GRAD, range(2, 3))
-    matrix(write_to(gmat))
-
-    from_matrix(lambda columns: nn(gmat[...], permuted[:, columns]))
-    turn_back(BACK_L, whole)
+    left_gradient(two)
     z_start_back(B0)
-
-    def columns_of(part):
-        gts[part, :, :ROWS] = nt(order[part], gmat[...]).astype(BF16)
-
     loop(S, columns_of)
-
-    def give(d):
-        return s_copy(2, gts.at[mate(d)], gtr.at[s], s, mate(d))
-
-    loop(S - 1, lambda d: give(d).start())
-    gtr[s] = gts[s]
+    loop(S - 1, lambda d: give(0, d).start())
+    z_wait(G2)
+    left_gradient(last)
+    z_start_back(B1)
+    loop(S, last_columns_of)
+    loop(S - 1, lambda d: give(1, d).start())
+    gtr0[s] = gts0[s]
+    gtr1[s] = gts1[s]
     early[1]()
-    s_wait(1, left, mate(0))
-    s_wait(1, left, mate(2))
-    loop(S - 1, lambda d: s_wait(2, gtr, mate(d)))
+    for d in (0, 2):
+        s_wait(2, left, mate(d), full)
+    loop(S - 1, lambda d: s_wait(3, gtr0, mate(d), full))
+    loop(S - 1, lambda d: s_wait(4, gtr1, mate(d), full))
+
+    def join(part):
+        gs[part, :, :128] = gtr0[part]
+        gs[part, :, 128:ROWS] = gtr1[part, :, :64]
+
+    loop(S, join)
     from_matrix(
-        lambda columns: sum(nn(gtr[k, :, :ROWS], left[k, :, columns]) for k in range(S))
+        whole,
+        lambda kept, columns: sum(nn(gs[k, :, :ROWS], left[k, :, columns]) for k in range(S)),
     )
-    turn_back(BACK_R, whole)
-    z_start_back(B1)
+    turn_back(BACK_R, two)
     z_start_back(B2)
+    turn_back(BACK_R, last)
+    z_start_back(B3)
     early[2]()
 
     def grads_of(array, phase, first, block_first, count):
         def body(step):
             block, own = block_first + step, first + step
             values = jnp.concatenate([yr[phase][k, own] for k in range(G)], axis=0)
-            upstream = values.astype(F32) * mask_ref[block]
+            grad = values.astype(F32) * mask_ref[block]
             row = 2 * array * C
             value = proj[block, row : row + C]
             gate = jax.nn.sigmoid(proj[block, row + C : row + 2 * C])
-            pieces = (upstream * gate, upstream * value * gate * (1.0 - gate))
+            pieces = (grad * gate, grad * value * gate * (1.0 - gate))
             for k in range(2):
                 piece = pieces[k].astype(BF16)
                 columns = slice(row + k * C, row + (k + 1) * C)
@@ -588,22 +656,26 @@
 
     z_wait(B0)
     y_start_back(B0)
+    z_wait(B1)
+    y_start_back(B1)
     early[3]()
     y_wait(B0)
-    grads_of(0, B0, 0, 0, 8)
-    z_wait(B1)
-    y_start_back(B1)
+    grads_of(0, B0, 0, 0, 6)
     y_wait(B1)
-    grads_of(0, B1, 0, 8, 1)
+    grads_of(0, B1, 0, 6, 2)
+    z_wait(B2)
+    y_start_back(B2)
+    y_wait(B2)
+    grads_of(0, B2, 0, 8, 1)
     middle = summing(1, 0)
     middle[0]()
-    grads_of(1, B1, 1, 0, 5)
-    z_wait(B2)
-    y_start_back(B2)
+    grads_of(1, B2, 1, 0, 5)
+    z_wait(B3)
+    y_start_back(B3)
     early[4]()
     middle[1]()
-    y_wait(B2)
-    grads_of(1, B2, 0, 5, 4)
+    y_wait(B3)
+    grads_of(1, B3, 0, 5, 4)
     late = summing(2, 2)
     late[0]()
     middle[2]()
@@ -633,11 +705,13 @@
     for phase in range(len(PHASES)):
         loop(G - 1, lambda d, p=phase: y_copy(p, next_g(d), g).wait_send())
         loop(Z - 1, lambda d, p=phase: z_copy(p, next_z(d), z).wait_send())
-    for phase, ref in enumerate((right, left)):
+    for phase, (ref, rows) in enumerate(((right, most), (right, least), (left, full))):
         for d in range(2):
-            s_copy(phase, ref.at[s], ref.at[s], s, mate(d)).wait_send()
-        passing_on(phase, ref).wait_send()
-    loop(S - 1, lambda d: give(d).wait_send())
+            part = ref.at[s, rows]
+            s_copy(phase, part, part, s, mate(d)).wait_send()
+        passing_on(phase, ref, rows).wait_send()
+    for which in range(2):
+        loop(S - 1, lambda d, w=which: give(w, d).wait_send())
     early[5]()
     middle[5]()
     late[5]()
@@ -689,8 +763,12 @@
             pltpu.VMEM((S, ROWS, WIDE), BF16),
             pltpu.VMEM((WIDE, WIDE), BF16),
             pltpu.VMEM((ROWS, WIDE), BF16),
-            *[pltpu.VMEM((S, ROWS, 256), BF16)] * 4,
+            pltpu.VMEM((8, S * ROWS, C), F32),
+            pltpu.VMEM((S, ROWS, 256), BF16),
+            *[pltpu.VMEM((S, ROWS, C), BF16)] * 4,
             pltpu.VMEM((C, 6 * C), F32),
+            pltpu.VMEM((BLOCKS, C, C), F32),
+            pltpu.VMEM((BLOCKS, C, C), F32),
             *y_buffers,
             *y_buffers,
             *z_buffers,
@@ -699,7 +777,7 @@
             *[buffer for _ in range(3) for buffer in sum_buffers()],
             *sems(len(PHASES), G),
             *sems(len(PHASES), Z),
-            *sems(3, S),
+            *sems(5, S),
             *[sem for _ in range(3) for n in (Z, G, S, Z) for sem in sems(n)],
             pltpu.SemaphoreType.DMA((6,)),
         ],

time: 181 us -> 176 us (0.972)
  Pallas kernels: 174 us -> 169 us
    pallas_call x1, Pallas kernels: 174 us -> 169 us  [on_device(): pl.pallas_call(kernel, out_shape=(jax.ShapeDtypeStruct((pixels, C), BF16)...]
where the time goes in v4:
time: 176 us; the launch traced here: 175 us
  Pallas kernels  169 us (96%)
  local copies, waits for them, and re-layouts  5.3 us (3%)
    pallas_call x1, Pallas kernels, on_device(): pl.pallas_call(kernel, out_shape=(jax.ShapeDtypeStruct((pixels, C), BF16)...  169 us
    unnamed x5, local copies, waits for them, and re-layouts  4.42 us

profile of v4, /device:TPU:1, one launch (start us, length us, event | category | flops | bytes accessed | tf_op | source)
XLA Modules:
  0.0 175.2 jit_solution(4478476343885945842)
XLA Ops:
  0.6 0.7 convert_element_type.3
  1.3 0.1 reshape.26
  1.4 0.1 copy.9
  1.5 0.7 reshape.30.mask_ref
  2.2 168.6 %shard_map.76 = (bf16[1152,128]{1,0:T(8,128)(2,1)}, f32[1152,128]{1,0:T(8,128)}, f32[6,128,128]{2,1,0:T(8,128)}) custom-call(bf16[1152,128]{1,0:T(8,128)(2,1)} %bitcast.11, bf16[1152,128]{1,0:T(8,128)(2,1)} %bitcast.12, bf16[4,192,1024]{2,1,0:T(8,128)(2,1)} %constant.2.clone.order_hbm, f32[9,1,128]{2,1,0:T(1,128)} %reshape.30.mask_ref, ...), custom_call_target="tpu_custom_call" | custom-call | tf_op jit(solution)/shard_map/pallas_call | solution.py:737
  170.8 0.0 copy-start
  170.8 1.8 %copy.14 = bf16[48,24,128]{2,1,0:T(8,128)(2,1)} copy(bf16[48,24,128]{2,1,0:T(8,128)(2,1)} %bitcast.10) | data formatting | bytes 589824
  172.6 1.9 %copy.15 = f32[48,24,128]{2,1,0:T(8,128)} copy(f32[48,24,128]{2,1,0:T(8,128)} %bitcast.9) | data formatting | bytes 1179648
  174.5 0.0 copy-done
  174.5 0.7 copy.16
Async XLA Ops:
  170.8 3.7 %copy-start = (f32[6,128,128]{2,1,0:T(8,128)S(1)}, f32[6,128,128]{2,1,0:T(8,128)}, u32[]{:S(2)}) copy-start(f32[6,128,128]{2,1,0:T(8,128)} %get-tuple-element.14) | copy-start | bytes 1179652

commit v5 on v4

--- a/solution.py
+++ b/solution.py
@@ -131,7 +131,7 @@
     ys, yr, zs, zr, flats = ([rest.pop(0) for _ in PHASES] for _ in range(5))
     sums = [[rest.pop(0) for _ in range(8)] for _ in range(3)]
     y_send, y_recv, z_send, z_recv, s_send, s_recv = (rest.pop(0) for _ in range(6))
-    w_sems = [[rest.pop(0) for _ in range(8)] for _ in range(3)]
+    w_sems = [rest.pop(0) for _ in range(3)]
     local = rest.pop(0)
 
     r = lax.axis_index("row")
@@ -176,12 +176,23 @@
     load_cot.start()
     load_order.start()
 
+    def all_of(ref, count, send_sem, recv_sem):
+        part = ref.at[pl.ds(0, count)]
+        return pltpu.make_async_remote_copy(
+            src_ref=part,
+            dst_ref=part,
+            send_sem=send_sem,
+            recv_sem=recv_sem,
+            device_id=along(next_z(0)),
+            device_id_type=MESH,
+        )
+
     def y_copy(phase, to, slot):
         return pltpu.make_async_remote_copy(
             src_ref=ys[phase].at[to],
             dst_ref=yr[phase].at[slot],
-            send_sem=y_send.at[phase, to],
-            recv_sem=y_recv.at[phase, slot],
+            send_sem=y_send.at[phase],
+            recv_sem=y_recv.at[phase],
             device_id=group(to),
             device_id_type=MESH,
         )
@@ -190,18 +201,24 @@
         loop(G - 1, lambda d: y_copy(phase, next_g(d), g).start())
         yr[phase][g] = ys[phase][g]
 
+    def y_all(phase):
+        return all_of(yr[phase], G - 1, y_send.at[phase], y_recv.at[phase])
+
     def y_wait(phase):
-        loop(G - 1, lambda d: y_copy(phase, next_g(d), next_g(d)).wait_recv())
+        y_all(phase).wait_recv()
 
     def z_copy(phase, to, slot):
         return pltpu.make_async_remote_copy(
             src_ref=zs[phase].at[to],
             dst_ref=zr[phase].at[slot],
-            send_sem=z_send.at[phase, to],
-            recv_sem=z_recv.at[phase, slot],
+            send_sem=z_send.at[phase],
+            recv_sem=z_recv.at[phase],
             device_id=along(to),
             device_id_type=MESH,
         )
+
+    def z_all(phase):
+        return all_of(zr[phase], Z - 1, z_send.at[phase], z_recv.at[phase])
 
     def z_start(phase, make):
         def send(step):
@@ -216,16 +233,12 @@
         rows = HELD[phase]
         flat = flats[phase]
 
-        def receive(step):
-            frm = next_z(Z - 2 - step)
-            z_copy(phase, frm, frm).wait_recv()
-
         def widen(step):
             for k in range(4):
                 frm = step * 4 + k
                 flat[at(frm * (rows // 16), rows, 16), :] = zr[phase][frm].astype(F32)
 
-        loop(Z - 1, receive)
+        z_all(phase).wait_recv()
         loop(Z // 4, widen)
 
     def y_fill(phase):
@@ -250,13 +263,18 @@
     def y_start_back(phase):
         blocks, rows = len(PHASES[phase]), HELD[phase]
 
-        def body(k):
-            for other in range(G):
+        def fill(other):
+            for k in range(blocks):
                 values = flats[phase][pl.ds(other * blocks + k, Z, stride=rows), :]
                 ys[phase][other, k] = values.astype(BF16)
 
-        loop(blocks, body)
-        y_start(phase)
+        def send(d):
+            fill(next_g(d))
+            y_copy(phase, next_g(d), g).start()
+
+        loop(G - 1, send)
+        fill(g)
+        yr[phase][g] = ys[phase][g]
 
     def place(array, block, part):
         phase, k = WHERE[array, block]
@@ -354,8 +372,8 @@
             return pltpu.make_async_remote_copy(
                 src_ref=src,
                 dst_ref=dst,
-                send_sem=sems[2 * step].at[to],
-                recv_sem=sems[2 * step + 1].at[slot],
+                send_sem=sems.at[step, 0],
+                recv_sem=sems.at[step, 1],
                 device_id=device,
                 device_id_type=MESH,
             )
@@ -373,9 +391,13 @@
             count, other = others[step]
             loop(count, lambda d: copies[step](other(d), mine[step]).start())
 
+        def every(step):
+            return all_of(
+                (a_r, b_r, c_r, d_r)[step], others[step][0], sems.at[step, 0], sems.at[step, 1]
+            )
+
         def wait(step):
-            count, other = others[step]
-            loop(count, lambda d: copies[step](other(d), other(d)).wait_recv())
+            every(step).wait_recv()
 
         def one():
             for k in range(Z):
@@ -408,16 +430,16 @@
                 gw_ref[first + k // 8, (k % 8) * 16 : (k % 8) * 16 + 16] = d_r[k].astype(F32)
 
         def sent():
-            for step, (count, other) in enumerate(others):
-                loop(count, lambda d, c=copies[step], o=other: c(o(d), o(d)).wait_send())
+            for step in range(len(others)):
+                every(step).wait_send()
 
         return one, two, three, four, five, sent
 
-    for m in range(6):
+    def turn_weight(m):
         wt[m * C : (m + 1) * C] = weights_ref[m].astype(F32).T.astype(BF16)
-    for m in range(5):
-        wback[:, m * C : (m + 1) * C] = weights_ref[m]
-    gwin[...] = jnp.zeros_like(gwin)
+
+    for m in (2, 3):
+        turn_weight(m)
 
     def tile_rows(ref, row):
         return ref[at(row, TILE_ROWS, TILE_ROWS), :].astype(F32).reshape(16, 24, C)
@@ -455,6 +477,8 @@
     pl.semaphore_wait(barrier, Z + G + S - 3)
 
     y_start(A0)
+    for m in (0, 1):
+        turn_weight(m)
     loop(BLOCKS, lambda block: activate(block, 0))
     y_fill(A1)
     y_start(A1)
@@ -470,7 +494,12 @@
     z_start_up(A2)
     y_wait(A3)
     z_start_up(A3)
+    for m in (4, 5):
+        turn_weight(m)
     loop(BLOCKS, project_gate)
+    for m in range(5):
+        wback[:, m * C : (m + 1) * C] = weights_ref[m]
+    gwin[...] = jnp.zeros_like(gwin)
     load_cot.wait()
 
     def turn_cotangent(row):
@@ -588,8 +617,6 @@
     pass_on(2, left, full)
 
     def left_gradient(rows):
-        turn_up(GRAD, rows)
-        matrix(gmat, rows)
         from_matrix(rows, lambda kept, columns: nn(gmat[kept], permuted[:, columns]))
         turn_back(BACK_L, rows)
 
@@ -605,15 +632,19 @@
 
     z_wait(G0)
     z_wait(G1)
+    turn_up(GRAD, two)
+    matrix(gmat, two)
     left_gradient(two)
     z_start_back(B0)
     loop(S, columns_of)
     loop(S - 1, lambda d: give(0, d).start())
     z_wait(G2)
+    turn_up(GRAD, last)
+    matrix(gmat, last)
+    loop(S, last_columns_of)
+    loop(S - 1, lambda d: give(1, d).start())
     left_gradient(last)
     z_start_back(B1)
-    loop(S, last_columns_of)
-    loop(S - 1, lambda d: give(1, d).start())
     gtr0[s] = gts0[s]
     gtr1[s] = gts1[s]
     early[1]()
@@ -703,8 +734,8 @@
     store_upd.wait()
     loop(3, lambda row: store_gpair(row).wait())
     for phase in range(len(PHASES)):
-        loop(G - 1, lambda d, p=phase: y_copy(p, next_g(d), g).wait_send())
-        loop(Z - 1, lambda d, p=phase: z_copy(p, next_z(d), z).wait_send())
+        y_all(phase).wait_send()
+        z_all(phase).wait_send()
     for phase, (ref, rows) in enumerate(((right, most), (right, least), (left, full))):
         for d in range(2):
             part = ref.at[s, rows]
@@ -715,6 +746,22 @@
     early[5]()
     middle[5]()
     late[5]()
+
+
+def hand_over(a, b, c, a_out, b_out, c_out, a_v, b_v, c_v, sems):
+    held = (a_v, b_v, c_v)
+    ins = [pltpu.make_async_copy(x, v, sems.at[k]) for k, (x, v) in enumerate(zip((a, b, c), held))]
+    outs = [
+        pltpu.make_async_copy(v, x, sems.at[3 + k])
+        for k, (x, v) in enumerate(zip((a_out, b_out, c_out), held))
+    ]
+    for copy in ins:
+        copy.start()
+    for k in range(3):
+        ins[k].wait()
+        outs[k].start()
+    for copy in outs:
+        copy.wait()
 
 
 def on_device(pair, pair_mask, weights, cotangent):
@@ -775,10 +822,10 @@
             *z_buffers,
             *[pltpu.VMEM((Z * rows, C), F32) for rows in HELD],
             *[buffer for _ in range(3) for buffer in sum_buffers()],
-            *sems(len(PHASES), G),
-            *sems(len(PHASES), Z),
+            *sems(len(PHASES)),
+            *sems(len(PHASES)),
             *sems(5, S),
-            *[sem for _ in range(3) for n in (Z, G, S, Z) for sem in sems(n)],
+            *[pltpu.SemaphoreType.DMA((4, 2))] * 3,
             pltpu.SemaphoreType.DMA((6,)),
         ],
         compiler_params=pltpu.CompilerParams(
@@ -791,6 +838,17 @@
         mask,
         weights,
     )
+    results = (update, grad_pair, grad_weights)
+    update, grad_pair, grad_weights = pl.pallas_call(
+        hand_over,
+        out_shape=tuple(jax.ShapeDtypeStruct(a.shape, a.dtype) for a in results),
+        in_specs=[anywhere] * 3,
+        out_specs=(anywhere,) * 3,
+        scratch_shapes=[
+            *[pltpu.VMEM(a.shape, a.dtype) for a in results],
+            pltpu.SemaphoreType.DMA((6,)),
+        ],
+    )(*results)
     return update.reshape(pair.shape), grad_pair.reshape(pair.shape), grad_weights
 
 

time: 176 us -> 157 us (0.89)
  Pallas kernels: 169 us -> 155 us
  local copies, waits for them, and re-layouts: 5.3 us -> 0.88 us
    pallas_call x1, Pallas kernels: 169 us -> 152 us  [on_device(): pl.pallas_call(kernel, out_shape=(jax.ShapeDtypeStruct((pixels, C), BF16)...]
    unnamed x5 -> x0, local copies, waits for them, and re-layouts: 4.42 us -> none
    pallas_call x0 -> x1, Pallas kernels: none -> 2.15 us  [on_device(): pl.pallas_call(hand_over, out_shape=tuple((jax.ShapeDtypeStruct(a.shape,...]
where the time goes in v5:
time: 157 us
  Pallas kernels  155 us (99%)
    pallas_call x1, Pallas kernels, on_device(): pl.pallas_call(kernel, out_shape=(jax.ShapeDtypeStruct((pixels, C), BF16)...  152 us

profile of v5, /device:TPU:1, one launch (start us, length us, event | category | flops | bytes accessed | tf_op | source)
XLA Modules:
  0.0 156.9 jit_solution(16907080308494214413)
XLA Ops:
  0.6 0.7 convert_element_type.3
  1.3 0.1 reshape.26
  1.4 0.1 copy.9
  1.5 0.7 reshape.30.mask_ref
  2.2 152.5 %shard_map.76 = (bf16[1152,128]{1,0:T(8,128)(2,1)}, f32[1152,128]{1,0:T(8,128)}, f32[6,128,128]{2,1,0:T(8,128)}) custom-call(bf16[1152,128]{1,0:T(8,128)(2,1)} %bitcast.9, bf16[1152,128]{1,0:T(8,128)(2,1)} %bitcast.10, bf16[4,192,1024]{2,1,0:T(8,128)(2,1)} %constant.2.clone.order_hbm, f32[9,1,128]{2,1,0:T(1,128)} %reshape.30.mask_ref, ...), custom_call_target="tpu_custom_call" | custom-call | tf_op jit(solution)/shard_map/pallas_call | solution.py:784
  154.7 2.1 %shard_map.77 = (bf16[1152,128]{1,0:T(8,128)(2,1)}, f32[1152,128]{1,0:T(8,128)}, f32[6,128,128]{2,1,0:T(8,128)}) custom-call(bf16[1152,128]{1,0:T(8,128)(2,1)} %get-tuple-element.9.a, f32[1152,128]{1,0:T(8,128)} %get-tuple-element.10.b, f32[6,128,128]{2,1,0:T(8,128)} %get-tuple-element.11.c), custom_call_target="tpu_custom_call" | custom-call | tf_op jit(solution)/shard_map/pallas_call | solution.py:842

commit v6 on v5

--- a/solution.py
+++ b/solution.py
@@ -11,13 +11,13 @@
 BF16 = jnp.bfloat16
 C = 128
 BLOCKS = 9
-Y, S, Z, G = 4, 4, 16, 8
+Y, S, Z, G, W = 4, 4, 16, 8, 32
 ROWS = 192
 WIDE = 1024
 TILE_ROWS = 384
 MESH = pl.DeviceIdType.MESH
 RIGHT, LEFT, TRI, GRAD, BACK_L, BACK_R = range(6)
-A0, A1, A2, A3, T0, T1, T2, G0, G1, G2, B0, B1, B2, B3 = range(14)
+A0, A1, A2, A3, A4, T0, T1, T2, G0, G1, G2, B0, B1, B2, B3 = range(15)
 
 
 def some(array, first, last):
@@ -28,7 +28,8 @@
     some(RIGHT, 0, 6),
     some(RIGHT, 6, 9) + some(LEFT, 0, 1),
     some(LEFT, 1, 3),
-    some(LEFT, 3, 9),
+    some(LEFT, 3, 7),
+    some(LEFT, 7, 9),
     some(TRI, 0, 2),
     some(TRI, 2, 6),
     some(TRI, 6, 9),
@@ -77,6 +78,11 @@
 
 
 def loop(count, body):
+    if count <= 9:
+        for i in range(count):
+            body(i)
+        return
+
     def step(i, carry):
         body(i)
         return carry
@@ -129,7 +135,7 @@
 ):
     rest = list(rest)
     ys, yr, zs, zr, flats = ([rest.pop(0) for _ in PHASES] for _ in range(5))
-    sums = [[rest.pop(0) for _ in range(8)] for _ in range(3)]
+    sums = [[rest.pop(0) for _ in range(6)] for _ in range(3)]
     y_send, y_recv, z_send, z_recv, s_send, s_recv = (rest.pop(0) for _ in range(6))
     w_sems = [rest.pop(0) for _ in range(3)]
     local = rest.pop(0)
@@ -139,6 +145,7 @@
     y, s = r // 4, r % 4
     half, z = q // 16, q % 16
     g = y * 2 + half
+    w = g * S + s
 
     def group(other):
         return {"row": (other // 2) * 4 + s, "col": (other % 2) * 16 + z}
@@ -154,6 +161,12 @@
 
     def next_g(d):
         return (g + 1 + d) % G
+
+    def across(other):
+        return {"row": (other // 8) * 4 + other % 4, "col": (other // 4 % 2) * 16 + z}
+
+    def next_w(d):
+        return (w + 1 + d) % W
 
     def next_z(step):
         t = Z - 1 - step
@@ -166,8 +179,7 @@
         pl.semaphore_signal(barrier, inc=1, device_id=device, device_id_type=MESH)
 
     loop(Z - 1, lambda d: greet(along(next_z(d))))
-    loop(G - 1, lambda d: greet(group(next_g(d))))
-    loop(S - 1, lambda d: greet(shared(mate(d))))
+    loop(W - 1, lambda d: greet(across(next_w(d))))
 
     load_pair = pltpu.make_async_copy(pair_hbm, pair_v, local.at[0])
     load_cot = pltpu.make_async_copy(cot_hbm, cot_v, local.at[1])
@@ -365,7 +377,7 @@
         passing_on(phase, ref, rows).start()
 
     def summing(which, first):
-        a_s, a_r, b_s, b_r, c_s, c_r, d_s, d_r = sums[which]
+        a_s, a_r, b_s, b_r, c_s, c_r = sums[which]
         sems = w_sems[which]
 
         def copy(step, src, dst, to, slot, device):
@@ -379,13 +391,12 @@
             )
 
         copies = (
-            lambda to, slot: copy(0, a_s.at[to], a_r.at[slot], to, slot, along(to)),
-            lambda to, slot: copy(1, b_s, b_r.at[slot], to, slot, group(to)),
-            lambda to, slot: copy(2, c_s, c_r.at[slot], to, slot, shared(to)),
-            lambda to, slot: copy(3, d_s, d_r.at[slot], to, slot, along(to)),
+            lambda to, slot: copy(0, a_s.at[to], a_r.at[slot], to, slot, across(to)),
+            lambda to, slot: copy(1, b_s, b_r.at[slot], to, slot, along(to)),
+            lambda to, slot: copy(2, c_s, c_r.at[slot], to, slot, across(to)),
         )
-        others = ((Z - 1, next_z), (G - 1, next_g), (S - 1, mate), (Z - 1, next_z))
-        mine = (z, g, s, z)
+        others = ((W - 1, next_w), (Z - 1, next_z), (W - 1, next_w))
+        mine = (w, z, w)
 
         def start(step):
             count, other = others[step]
@@ -393,47 +404,41 @@
 
         def every(step):
             return all_of(
-                (a_r, b_r, c_r, d_r)[step], others[step][0], sems.at[step, 0], sems.at[step, 1]
+                (a_r, b_r, c_r)[step], others[step][0], sems.at[step, 0], sems.at[step, 1]
             )
 
         def wait(step):
             every(step).wait_recv()
 
         def one():
-            for k in range(Z):
-                rows, columns = (k % 8) * 16, (first + k // 8) * C
-                a_s[k] = gwin[rows : rows + 16, columns : columns + C].astype(BF16)
+            for k in range(W):
+                rows, columns = (k % 16) * 8, (first + k // 16) * C
+                a_s[k] = gwin[rows : rows + 8, columns : columns + C]
             start(0)
-            a_r[z] = a_s[z]
+            a_r[w] = a_s[w]
 
         def two():
             wait(0)
-            b_s[...] = sum(a_r[k].astype(F32) for k in range(Z))
+            b_s[...] = sum(a_r[k] for k in range(W))
             start(1)
-            b_r[g] = b_s[...]
+            b_r[z] = b_s[...]
 
         def three():
             wait(1)
-            c_s[...] = sum(b_r[k] for k in range(G))
+            c_s[...] = sum(b_r[k] for k in range(Z)) * (1.0 / 768.0)
             start(2)
-            c_r[s] = c_s[...]
+            c_r[w] = c_s[...]
 
         def four():
             wait(2)
-            d_s[...] = (sum(c_r[k] for k in range(S)) * (1.0 / 768.0)).astype(BF16)
-            start(3)
-            d_r[z] = d_s[...]
-
-        def five():
-            wait(3)
-            for k in range(Z):
-                gw_ref[first + k // 8, (k % 8) * 16 : (k % 8) * 16 + 16] = d_r[k].astype(F32)
+            for k in range(W):
+                gw_ref[first + k // 16, (k % 16) * 8 : (k % 16) * 8 + 8] = c_r[k]
 
         def sent():
             for step in range(len(others)):
                 every(step).wait_send()
 
-        return one, two, three, four, five, sent
+        return one, two, three, four, sent
 
     def turn_weight(m):
         wt[m * C : (m + 1) * C] = weights_ref[m].astype(F32).T.astype(BF16)
@@ -474,7 +479,7 @@
 
     loop(3, project_right)
     y_fill(A0)
-    pl.semaphore_wait(barrier, Z + G + S - 3)
+    pl.semaphore_wait(barrier, Z + W - 2)
 
     y_start(A0)
     for m in (0, 1):
@@ -484,16 +489,20 @@
     y_start(A1)
     y_fill(A2)
     y_fill(A3)
+    y_fill(A4)
     y_wait(A0)
     z_start_up(A0)
     y_start(A2)
     y_wait(A1)
     z_start_up(A1)
     y_start(A3)
+    y_start(A4)
     y_wait(A2)
     z_start_up(A2)
     y_wait(A3)
     z_start_up(A3)
+    y_wait(A4)
+    z_start_up(A4)
     for m in (4, 5):
         turn_weight(m)
     loop(BLOCKS, project_gate)
@@ -554,10 +563,13 @@
     triangle(range(1))
     z_start_back(T0)
     z_wait(A3)
-    turn_up(LEFT, range(1, 3))
-    matrix(left.at[s], range(1, 3))
+    turn_up(LEFT, range(1, 2))
+    matrix(left.at[s], range(1, 2))
     triangle(range(1, 2))
     z_start_back(T1)
+    z_wait(A4)
+    turn_up(LEFT, last)
+    matrix(left.at[s], last)
     triangle(last)
     z_start_back(T2)
 
@@ -703,7 +715,6 @@
     grads_of(1, B2, 1, 0, 5)
     z_wait(B3)
     y_start_back(B3)
-    early[4]()
     middle[1]()
     y_wait(B3)
     grads_of(1, B3, 0, 5, 4)
@@ -728,8 +739,6 @@
     middle[3]()
     late[2]()
     late[3]()
-    middle[4]()
-    late[4]()
 
     store_upd.wait()
     loop(3, lambda row: store_gpair(row).wait())
@@ -743,9 +752,9 @@
         passing_on(phase, ref, rows).wait_send()
     for which in range(2):
         loop(S - 1, lambda d, w=which: give(w, d).wait_send())
-    early[5]()
-    middle[5]()
-    late[5]()
+    early[4]()
+    middle[4]()
+    late[4]()
 
 
 def hand_over(a, b, c, a_out, b_out, c_out, a_v, b_v, c_v, sems):
@@ -774,10 +783,13 @@
         return [pltpu.SemaphoreType.DMA(shape)] * 2
 
     def sum_buffers():
-        one = [pltpu.VMEM((16, C), F32), pltpu.VMEM((G, 16, C), F32)]
-        two = [pltpu.VMEM((16, C), F32), pltpu.VMEM((S, 16, C), F32)]
-        last = [pltpu.VMEM((16, C), BF16), pltpu.VMEM((Z, 16, C), BF16)]
-        return [pltpu.VMEM((Z, 16, C), BF16)] * 2 + one + two + last
+        return [
+            *[pltpu.VMEM((W, 8, C), F32)] * 2,
+            pltpu.VMEM((8, C), F32),
+            pltpu.VMEM((Z, 8, C), F32),
+            pltpu.VMEM((8, C), F32),
+            pltpu.VMEM((W, 8, C), F32),
+        ]
 
     y_buffers = [pltpu.VMEM((G, len(items), 16, C), BF16) for items in PHASES]
     z_buffers = [pltpu.VMEM((Z, rows, C), BF16) for rows in HELD]
@@ -825,7 +837,7 @@
             *sems(len(PHASES)),
             *sems(len(PHASES)),
             *sems(5, S),
-            *[pltpu.SemaphoreType.DMA((4, 2))] * 3,
+            *[pltpu.SemaphoreType.DMA((3, 2))] * 3,
             pltpu.SemaphoreType.DMA((6,)),
         ],
         compiler_params=pltpu.CompilerParams(

time: 157 us -> 151 us (0.962)
  Pallas kernels: 155 us -> 149 us
    pallas_call x1, Pallas kernels: 152 us -> 147 us  [on_device(): pl.pallas_call(kernel, out_shape=(jax.ShapeDtypeStruct((pixels, C), BF16)...]
where the time goes in v6:
time: 151 us
  Pallas kernels  149 us (99%)
    pallas_call x1, Pallas kernels, on_device(): pl.pallas_call(kernel, out_shape=(jax.ShapeDtypeStruct((pixels, C), BF16)...  147 us

profile of v6, /device:TPU:1, one launch (start us, length us, event | category | flops | bytes accessed | tf_op | source)
XLA Modules:
  0.0 151.0 jit_solution(5925398939016249603)
XLA Ops:
  0.6 0.7 convert_element_type.3
  1.3 0.1 reshape.26
  1.4 0.1 copy.9
  1.5 0.7 reshape.30.mask_ref
  2.2 146.6 %shard_map.76 = (bf16[1152,128]{1,0:T(8,128)(2,1)}, f32[1152,128]{1,0:T(8,128)}, f32[6,128,128]{2,1,0:T(8,128)}) custom-call(bf16[1152,128]{1,0:T(8,128)(2,1)} %bitcast.9, bf16[1152,128]{1,0:T(8,128)(2,1)} %bitcast.10, bf16[4,192,1024]{2,1,0:T(8,128)(2,1)} %constant.2.clone.order_hbm, f32[9,1,128]{2,1,0:T(1,128)} %reshape.30.mask_ref, ...), custom_call_target="tpu_custom_call" | custom-call | tf_op jit(solution)/shard_map/pallas_call | solution.py:796
  148.8 2.1 %shard_map.77 = (bf16[1152,128]{1,0:T(8,128)(2,1)}, f32[1152,128]{1,0:T(8,128)}, f32[6,128,128]{2,1,0:T(8,128)}) custom-call(bf16[1152,128]{1,0:T(8,128)(2,1)} %get-tuple-element.9.a, f32[1152,128]{1,0:T(8,128)} %get-tuple-element.10.b, f32[6,128,128]{2,1,0:T(8,128)} %get-tuple-element.11.c), custom_call_target="tpu_custom_call" | custom-call | tf_op jit(solution)/shard_map/pallas_call | solution.py:854
